TPU v7x, 32 devices: a whole 2x2x4 slice. The times are simulated.
32 devices in a mesh: leaf: 8 (over z, x), grp: 4 (over y, core).
Axes of the slice: x: 2, y: 2, z: 4, core: 2. Of those that a mesh axis runs over, the one named last changes fastest.
Arguments:
- vectors: float32 [16, 262144], P(None, ('leaf', 'grp')), may hold values from -6 to 6
- coords: float32 [2, 262144], P(None, ('leaf', 'grp')), may hold values from 0 to 1, as said below
- perm: int32 [262144], P(('leaf', 'grp')), may hold values from 0 to 8191, as said below
- bases: float32 [512, 64, 512], P(('leaf', 'grp')), may hold values from -0.25 to 0.25
- leaf_maps: float32 [512, 64, 64], P(('leaf', 'grp')), may hold values from -0.1875 to 0.1875
- node_maps: float32 [32, 64, 64], P(('leaf', 'grp')), may hold values from -0.375 to 0.375
- leaf_skel: float32 [512, 2, 64], P(('leaf', 'grp')), may hold values from 0 to 1
- node_skel: float32 [32, 2, 64], P(('leaf', 'grp')), may hold values from 0 to 1
- sub_skel: float32 [8, 2, 64], P('leaf'), may hold values from 0 to 1
- leaf_src: int32 [512, 16], P(('leaf', 'grp')), may hold values from 0 to 63
- leaf_count: int32 [512], P(('leaf', 'grp')), may hold values from 1 to 16
- node_src: int32 [32, 8], P(('leaf', 'grp')), may hold values from 0 to 11, as said below
- node_count: int32 [32], P(('leaf', 'grp')), may hold values from 1 to 8
Outputs:
- product: float32 [16, 262144], P(None, ('leaf', 'grp'))
Inputs may be any that keep to these rules, and one draw needn't show every extreme that they name: `perm`: each aligned block of 8192 entries holds every number of 0 to 8191 once. `coords`: rows 3k, 3k + 1 and 3k + 2 share one site's coordinates. `node_src`: entries index the device nodes of subtrees s - 1, s, s + 1 in order (s the node's own subtree), only subtrees that exist.
All inputs are finite; a program needn't handle non-finite values.
Results may differ from a plain program's by a relative error of at most 0.0003.
Values sent between devices are 32-bit elements; how exact they have to be, the bound alone decides.
No kernel may reach another device: no remote copies, remote signals or barrier semaphores. Data moves between devices by JAX's collectives and lax.ppermute only.
A program may use at most 64 MiB of HBM per device.

v0:
```python
import functools
import math

import jax
import jax.numpy as jnp
import numpy as np
from jax import lax
from jax.experimental import pallas as pl
from jax.experimental.pallas import tpu as pltpu
from jax.sharding import PartitionSpec as P

F32 = jnp.float32
BF16 = jnp.bfloat16
WIDE = 256
SHIFT = 8
LOG2E = math.log2(math.e)
TINY = 1e-37
PACK_ROWS = 24
PART = 32
AT_ONCE = 4


def make_tables(norm):
    smooth = [0, 2, 4]
    sigmas = [1.0, 0.8, 1.2]
    rho = [[1.0, 0.5, 0.3], [0.5, 1.0, 0.4], [0.3, 0.4, 1.0]]
    scale = np.zeros((3, 3))
    poly = np.zeros((5, 3, 3))
    for first in range(3):
        for second in range(3):
            order = (smooth[first] + smooth[second]) // 2
            scale[first, second] = -(2.0 * order + 1.0) * (LOG2E / 0.3) ** 2
            amp = sigmas[first] * sigmas[second] * rho[first][second] * norm
            for power in range(order + 1):
                kterm = order - power
                coeff = math.factorial(order) / math.factorial(2 * order)
                coeff = (
                    coeff
                    * math.factorial(order + kterm)
                    / (math.factorial(kterm) * math.factorial(order - kterm))
                )
                poly[power, first, second] = amp * coeff * 2.0**power * (-1.0 / LOG2E) ** power
    return scale, poly


def dot(one, two, turned=False):
    dims = (((1,), (1 if turned else 0,)), ((), ()))
    return lax.dot_general(one, two, dims, preferred_element_type=F32)


def parts(value):
    high = value.astype(BF16)
    return high, (value - high.astype(F32)).astype(BF16)


def product(one, two, turned=False):
    rows = one.shape[0]
    one_hi, one_lo = parts(one)
    two_hi, two_lo = parts(two)
    both = dot(jnp.concatenate([one_hi, one_lo], axis=0), two_hi, turned)
    return both[:rows] + both[rows:] + dot(one_hi, two_lo, turned)


def count_rows(rows):
    rows[...] = lax.broadcasted_iota(jnp.int32, rows.shape, 0).astype(jnp.int16)


def one_hot(rows, low):
    count = low.shape[1]
    low = jnp.broadcast_to(low, (16, count)).astype(jnp.int16)[None]
    same = rows[:, :count].reshape(WIDE // 16, 16, count) == low
    return jnp.where(same, jnp.bfloat16(1), jnp.bfloat16(0)).reshape(WIDE, count)


def fill(source, value, at, nvec):
    high, low = parts(value)
    source[pl.ds(at, nvec), :WIDE] = high
    source[pl.ds(at, nvec), WIDE:] = low


def pick(rows, source, index, nvec):
    count = index.shape[1]
    hot = one_hot(rows, index & (WIDE - 1))
    hot = jnp.concatenate([hot, hot], axis=0)
    chunk = jnp.broadcast_to(index >> SHIFT, (8, count))[None]
    out = jnp.zeros((nvec // 8, 8, count), F32)
    chunks = source.shape[0] // nvec
    found = dot(source[...], hot).reshape(chunks, nvec // 8, 8, count)
    for each in range(chunks):
        out = jnp.where(chunk == each, found[each], out)
    return out.reshape(nvec, count)


def leaf_index(perm, leaf, block):
    rows = block // 128
    return jnp.concatenate([perm[pl.ds(leaf * rows + each, 1), :] for each in range(rows)], axis=1)


def fetch(pairs, sems):
    copies = [pltpu.make_async_copy(src, dst, sems.at[each]) for each, (src, dst) in enumerate(pairs)]
    for copy in copies:
        copy.start()
    return copies


def up_kernel(*refs):
    given, (tree_out, leaf_pack, tree_pack) = refs[:8], refs[8:11]
    held = refs[11:19]
    tree_vec, source, rows, sems = refs[19:]
    count_rows(rows)
    copies = fetch(list(zip(given, held)), sems)
    vec, perm, bases, leaf_maps, node_maps, leaf_skel, node_skel, sub_skel = held
    leaves, nvec, block = tree_vec.shape
    rank = bases.shape[1]
    copies[0].wait()
    for each in range(vec.shape[1] // WIDE):
        fill(source, vec[:, each * WIDE : (each + 1) * WIDE], each * nvec, nvec)
    copies[1].wait()

    def gather(leaf, carry):
        tree_vec[leaf] = pick(rows, source, leaf_index(perm, leaf, block), nvec)
        return carry

    lax.fori_loop(0, leaves, gather, 0, unroll=2)
    leave = pltpu.make_async_copy(tree_vec, tree_out, sems.at[len(copies)])
    leave.start()
    for copy in copies[2:]:
        copy.wait()
    up_node = jnp.zeros((nvec, rank), F32)
    blank = jnp.zeros((PACK_ROWS - nvec - 2, 2 * rank), F32)
    for leaf in range(0, leaves, 2):
        up = [product(tree_vec[leaf + each], bases[leaf + each], True) for each in range(2)]
        leaf_pack[leaf // 2] = jnp.concatenate(
            [
                jnp.concatenate(up, axis=1),
                jnp.concatenate([leaf_skel[leaf], leaf_skel[leaf + 1]], axis=1),
                blank,
            ],
            axis=0,
        )
        for each in range(2):
            up_node = up_node + product(up[each], leaf_maps[leaf + each])
    up_sub = product(up_node, node_maps[0])
    packed = jnp.concatenate(
        [
            jnp.concatenate([up_node, up_sub], axis=1),
            jnp.concatenate([node_skel[0], sub_skel[0]], axis=1),
            blank,
        ],
        axis=0,
    )

    def spread(each, carry):
        tree_pack[each] = packed
        return carry

    lax.fori_loop(0, tree_pack.shape[0], spread, 0)
    leave.wait()


def near_kernel(shift, *refs):
    given, (near_out, inverse_out) = refs[:3], refs[3:5]
    held = refs[5:8]
    near, inverse, flat, source, rows, across, down, slots, sems = refs[8:]
    copies = fetch(list(zip(given, held)), sems)
    crd, perm, tree_vec = held
    count_rows(rows)
    leaves, nvec, block = tree_vec.shape
    chunks = crd.shape[1] // WIDE
    scale, poly = make_tables(1.0 / math.sqrt(block))
    slope = scale[0, 1] - scale[0, 0]
    copies[0].wait()
    for axis in range(2):
        for each in range(chunks):
            row = axis * chunks + each
            flat[row : row + 1, :] = crd[axis : axis + 1, each * WIDE : (each + 1) * WIDE]
    rest = flat[...]
    for piece in range(3):
        rounded = rest.astype(BF16)
        source[piece * 2 * chunks : (piece + 1) * 2 * chunks, :] = rounded
        rest = rest - rounded.astype(F32)
    slots[...] = jnp.zeros_like(slots)
    copies[1].wait()
    side = 128
    tiles = block // side

    def place_leaf(leaf, carry):
        index = leaf_index(perm, leaf, block)
        hot = one_hot(rows, index & (WIDE - 1))
        found = dot(source[...], hot)
        found = (
            found[: 2 * chunks] + found[2 * chunks : 4 * chunks] + found[4 * chunks :]
        )
        mine = lax.broadcasted_iota(jnp.int32, (chunks, block), 0) == index >> SHIFT
        lane = lax.broadcasted_iota(jnp.int32, (chunks, block), 1) + leaf * block
        lane_low = (lane & (WIDE - 1)).astype(F32)
        lane_high = (lane >> SHIFT).astype(F32)
        marks = jnp.concatenate(
            [jnp.where(mine, lane_low, 0.0), jnp.where(mine, lane_high, 0.0)], axis=0
        ).astype(BF16)
        slots[...] += dot(marks, hot, True)
        row_x = jnp.sum(jnp.where(mine, found[:chunks], 0.0), axis=0, keepdims=True)
        row_y = jnp.sum(jnp.where(mine, found[chunks:], 0.0), axis=0, keepdims=True)
        moved = index + shift[0]
        kind = moved - 3 * ((moved * 43691) >> 17)
        row_w = kind.astype(F32) * slope
        for place, row in enumerate((row_x, row_y, row_w)):
            across[leaf, place] = jnp.broadcast_to(row, (8, block))
            turned = jnp.transpose(jnp.broadcast_to(row, (side, block)))
            down[leaf, place] = turned.reshape(block // 8, 8, side)
        return carry

    lax.fori_loop(0, leaves, place_leaf, 0, unroll=2)
    inverse[...] = (slots[:chunks] + slots[chunks:] * WIDE).astype(jnp.int32)
    leave = pltpu.make_async_copy(inverse, inverse_out, sems.at[3])
    leave.start()
    copies[2].wait()

    def one_leaf(leaf, carry):
        vec_hi, vec_lo = parts(tree_vec[leaf])
        vec_both = jnp.concatenate([vec_hi, vec_lo], axis=0)
        total = [0.0] * tiles
        for col in reversed(range(tiles)):
            cols = slice(col * side, (col + 1) * side)
            over_x, over_y, over_w = [across[leaf, each, :, cols] for each in range(3)]
            over_zero, over_one = over_w > 0.5 * slope, over_w > 1.5 * slope

            def across_table(power, first):
                zero, one, two = [float(each) for each in poly[power, first]]
                return jnp.where(over_zero, zero, jnp.where(over_one, one, two))[None]

            table = [[across_table(power, first) for first in range(3)] for power in range(5)]
            over_w = (over_w + float(scale[0, 0]))[None]
            over_x, over_y = over_x[None], over_y[None]
            high, low = [], []
            for row in range((col + 1) * side // PART):
                at = slice(row * PART // 8, (row + 1) * PART // 8)
                diff_x = down[leaf, 0, at] - over_x
                diff_y = down[leaf, 1, at] - over_y
                down_w = down[leaf, 2, at]
                var_zero, var_one = down_w > 0.5 * slope, down_w > 1.5 * slope
                square = (diff_x * diff_x + diff_y * diff_y) * (down_w + over_w)
                arg = square * lax.rsqrt(TINY - square)
                value = jnp.where(var_one, 0.0, table[4][2])
                value = value * arg + jnp.where(
                    var_zero, 0.0, jnp.where(var_one, table[3][1], table[3][2])
                )
                for power in (2, 1, 0):
                    a, b, c = table[power]
                    value = value * arg + jnp.where(var_zero, a, jnp.where(var_one, b, c))
                value = (value * jnp.exp2(arg)).reshape(PART, side)
                value_hi, value_lo = parts(value)
                high.append(value_hi)
                low.append(value_lo)
            high = jnp.concatenate(high, axis=0)
            low = jnp.concatenate(low, axis=0)
            upto = (col + 1) * side
            both = dot(vec_both[:, :upto], high)
            direct = both[:nvec] + both[nvec:] + dot(vec_hi[:, :upto], low)
            total[col] = total[col] + direct
            if col > 0:
                both = dot(vec_both[:, cols], high[: col * side], True)
                back = both[:nvec] + both[nvec:] + dot(vec_hi[:, cols], low[: col * side], True)
                for row in range(col):
                    total[row] = total[row] + back[:, row * side : (row + 1) * side]
        for col in range(tiles):
            near[leaf, :, col * side : (col + 1) * side] = total[col]
        return carry

    lax.fori_loop(0, leaves, one_leaf, 0)
    leave.wait()
    leave = pltpu.make_async_copy(near, near_out, sems.at[3])
    leave.start()
    leave.wait()


def far_kernel(groups, subtrees, *refs):
    place, leaf_src, leaf_count, node_src, node_count = refs[:5]
    given, out_at = refs[5:16], refs[16]
    held = refs[17:28]
    source, coef, twice, cols, out, rows, srcs, dsts, sems = refs[28:]
    copies = fetch(list(zip(given, held)), sems)
    leaf_all, tree_all, leaf_skel, node_skel, sub_skel, tables = held[:6]
    leaf_maps, node_maps, bases, near, inverse = held[6:]
    count_rows(rows)
    leaves, nvec, block = near.shape
    rank = bases.shape[1]
    nodes = tree_all.shape[0]
    pairs = leaf_all.shape[0]
    node_at = 2 * pairs
    beside = 3 * groups
    sub_at = node_at + beside
    blank = sub_at + subtrees
    sub_pos = place[0]
    left = lax.broadcasted_iota(jnp.int32, (PACK_ROWS, 2 * rank), 1) < rank

    def list_leaf(leaf, at):
        count = leaf_count[leaf]

        def one(step, carry):
            srcs[2 * (at + step)] = leaf_src[leaf, 2 * step]
            second = jnp.where(2 * step + 1 < count, leaf_src[leaf, 2 * step + 1], blank)
            srcs[2 * (at + step) + 1] = second
            dsts[at + step] = leaf
            return carry

        steps = (count + 1) // 2
        lax.fori_loop(0, steps, one, 0)
        return at + steps

    size = lax.fori_loop(0, leaves, list_leaf, 0)
    count = node_count[0]

    def list_node(step, carry):
        srcs[2 * (size + step)] = node_at + node_src[0, 2 * step]
        second = jnp.where(2 * step + 1 < count, node_at + node_src[0, 2 * step + 1], blank)
        srcs[2 * (size + step) + 1] = second
        dsts[size + step] = leaves
        return carry

    steps = (count + 1) // 2
    lax.fori_loop(0, steps, list_node, 0)

    def list_sub(sub, at):
        srcs[at] = sub_at + sub
        dsts[at // 2] = leaves + 1
        return at + jnp.where(jnp.abs(sub - sub_pos) >= 2, 1, 0)

    ends = lax.fori_loop(0, subtrees, list_sub, 2 * (size + steps))
    srcs[ends] = blank
    dsts[ends // 2] = leaves + 1
    ends = (ends + 1) // 2
    for each in range(AT_ONCE):
        srcs[2 * (ends + each)] = blank
        srcs[2 * (ends + each) + 1] = blank
        dsts[ends + each] = leaves + 1

    copies[0].wait()

    def both_leaves(pair, carry):
        packs = leaf_all[pair]
        turned = pltpu.roll(packs, rank, 1)
        twice[2 * pair] = jnp.where(left, packs, turned)
        twice[2 * pair + 1] = jnp.where(left, turned, packs)
        return carry

    lax.fori_loop(0, pairs, both_leaves, 0, unroll=4)
    copies[1].wait()

    def both_node(each, carry):
        packs = tree_all[jnp.clip((sub_pos - 1) * groups + each, 0, nodes - 1)]
        twice[node_at + each] = jnp.where(left, packs, pltpu.roll(packs, rank, 1))
        return carry

    lax.fori_loop(0, beside, both_node, 0, unroll=4)

    def both_sub(sub, carry):
        total = tree_all[sub * groups, :nvec]
        for each in range(1, groups):
            total = total + tree_all[sub * groups + each, :nvec]
        packs = jnp.concatenate([total, tree_all[sub * groups, nvec:]], axis=0)
        twice[sub_at + sub] = jnp.where(left, pltpu.roll(packs, rank, 1), packs)
        return carry

    lax.fori_loop(0, subtrees, both_sub, 0, unroll=2)
    twice[blank] = jnp.zeros_like(twice[blank])
    coef[...] = jnp.zeros_like(coef)
    for copy in copies[2:6]:
        copy.wait()

    def upright(skel, at):
        for axis in range(2):
            row = jnp.broadcast_to(skel[axis : axis + 1], (2 * rank, rank))
            cols[at, axis] = jnp.transpose(row)

    def upright_leaf(leaf, carry):
        upright(leaf_skel[leaf], leaf)
        return carry

    lax.fori_loop(0, leaves, upright_leaf, 0, unroll=4)
    upright(node_skel[0], leaves)
    upright(sub_skel[0], leaves + 1)

    def couple(step, carry):
        terms = []
        for each in range(AT_ONCE):
            item = step * AT_ONCE + each
            packs = jnp.where(left, twice[srcs[2 * item]], twice[srcs[2 * item + 1]])
            target = dsts[item]
            diff_x = cols[target, 0] - packs[nvec : nvec + 1]
            diff_y = cols[target, 1] - packs[nvec + 1 : nvec + 2]
            square = (diff_x * diff_x + diff_y * diff_y) * tables[0]
            arg = square * lax.rsqrt(TINY - square)
            value = tables[5]
            for power in (4, 3, 2, 1):
                value = value * arg + tables[power]
            value = value * jnp.exp2(arg)
            terms.append((target, product(packs[:nvec], value, True)))
        for target, total in terms:
            coef[target] += total
        return carry

    lax.fori_loop(0, (ends + AT_ONCE - 1) // AT_ONCE, couple, 0)
    for copy in copies[6:]:
        copy.wait()
    down_node = coef[leaves] + product(coef[leaves + 1], node_maps[0], True)
    for leaf in range(leaves):
        down_leaf = coef[leaf] + product(down_node, leaf_maps[leaf], True)
        whole = near[leaf] + product(down_leaf, bases[leaf])
        for each in range(block // WIDE):
            fill(
                source,
                whole[:, each * WIDE : (each + 1) * WIDE],
                (leaf * (block // WIDE) + each) * nvec,
                nvec,
            )

    def scatter(each, carry):
        at = pl.multiple_of(each * 2 * WIDE, 2 * WIDE)
        index = jnp.concatenate(
            [inverse[pl.ds(2 * each, 1), :], inverse[pl.ds(2 * each + 1, 1), :]], axis=1
        )
        out[:, pl.ds(at, 2 * WIDE)] = pick(rows, source, index, nvec)
        return carry

    steps = inverse.shape[0] // 2
    segments = 4
    leaving = []
    for each in range(segments):
        start, stop = each * steps // segments, (each + 1) * steps // segments
        lax.fori_loop(start, stop, scatter, 0, unroll=2)
        span = slice(start * 2 * WIDE, stop * 2 * WIDE)
        leaving.append(pltpu.make_async_copy(out.at[:, span], out_at.at[:, span], sems.at[each]))
        leaving[-1].start()
    for copy in leaving:
        copy.wait()


def skeleton_tables(rank):
    scale, poly = make_tables(1.0 / math.sqrt(rank))
    var = np.arange(rank) % 3
    rows, cols = var[:, None], np.tile(var, 2)[None, :]
    return np.stack([scale[rows, cols]] + [poly[power][rows, cols] for power in range(5)]).astype(
        np.float32
    )


def shards(
    vectors,
    coords,
    perm,
    bases,
    leaf_maps,
    node_maps,
    leaf_skel,
    node_skel,
    sub_skel,
    leaf_src,
    leaf_count,
    node_src,
    node_count,
):
    nvec, rows_dev = vectors.shape
    leaves, rank, block = bases.shape
    groups = lax.axis_size("grp")
    subtrees = lax.axis_size("leaf")
    nodes = groups * subtrees
    sub_pos = lax.axis_index("leaf")
    device_pos = sub_pos * groups + lax.axis_index("grp")
    chunks = rows_dev // WIDE
    vmem = pl.BlockSpec(memory_space=pltpu.VMEM)
    smem = pl.BlockSpec(memory_space=pltpu.SMEM)
    hbm = pl.BlockSpec(memory_space=pltpu.HBM)
    anywhere = pl.BlockSpec(memory_space=pl.ANY)
    params = pltpu.CompilerParams(vmem_limit_bytes=60 * 1024 * 1024)
    order = perm.reshape(rows_dev // 128, 128)

    def like(*arrays):
        return [pltpu.VMEM(each.shape, each.dtype) for each in arrays]

    given = (vectors, order, bases, leaf_maps, node_maps, leaf_skel, node_skel, sub_skel)
    tree_vec, leaf_pack, tree_pack = pl.pallas_call(
        up_kernel,
        out_shape=(
            jax.ShapeDtypeStruct((leaves, nvec, block), F32),
            jax.ShapeDtypeStruct((leaves // 2, PACK_ROWS, 2 * rank), F32),
            jax.ShapeDtypeStruct((nodes, PACK_ROWS, 2 * rank), F32),
        ),
        in_specs=[hbm] * 8,
        out_specs=(hbm, vmem, vmem),
        scratch_shapes=like(*given)
        + [
            pltpu.VMEM((leaves, nvec, block), F32),
            pltpu.VMEM((chunks * nvec, 2 * WIDE), BF16),
            pltpu.VMEM((WIDE, block), jnp.int16),
            pltpu.SemaphoreType.DMA((9,)),
        ],
        compiler_params=params,
        name="up",
    )(*given)
    tree_all = lax.all_to_all(tree_pack, ("leaf", "grp"), 0, 0, tiled=True)
    leaf_all = lax.all_gather(leaf_pack, "grp", axis=0, tiled=True)
    shift = (device_pos * (rows_dev % 3) % 3).astype(jnp.int32).reshape(1)
    near, inverse = pl.pallas_call(
        near_kernel,
        out_shape=(
            jax.ShapeDtypeStruct((leaves, nvec, block), F32),
            jax.ShapeDtypeStruct((chunks, WIDE), jnp.int32),
        ),
        in_specs=[smem, hbm, hbm, hbm],
        out_specs=(hbm,) * 2,
        scratch_shapes=like(coords, order, tree_vec)
        + [
            pltpu.VMEM((leaves, nvec, block), F32),
            pltpu.VMEM((chunks, WIDE), jnp.int32),
            pltpu.VMEM((2 * chunks, WIDE), F32),
            pltpu.VMEM((6 * chunks, WIDE), BF16),
            pltpu.VMEM((WIDE, block), jnp.int16),
            pltpu.VMEM((leaves, 3, 8, block), F32),
            pltpu.VMEM((leaves, 3, block // 8, 8, 128), F32),
            pltpu.VMEM((2 * chunks, WIDE), F32),
            pltpu.SemaphoreType.DMA((4,)),
        ],
        compiler_params=params,
        cost_estimate=pl.CostEstimate(
            flops=128 * leaves * block * block,
            bytes_accessed=8 * leaves * nvec * block,
            transcendentals=leaves * block * block,
        ),
        name="near",
    )(shift, coords, order, tree_vec)
    tables = jnp.asarray(skeleton_tables(rank))
    given = (leaf_all, tree_all, leaf_skel, node_skel, sub_skel, tables)
    given = given + (leaf_maps, node_maps, bases, near, inverse)
    items = (leaf_src.size + node_src.size + subtrees + 2) // 2 + AT_ONCE
    sources = groups * leaves + 3 * groups + subtrees + 1
    return pl.pallas_call(
        functools.partial(far_kernel, groups, subtrees),
        out_shape=jax.ShapeDtypeStruct((nvec, rows_dev), F32),
        in_specs=[smem] * 5 + [hbm, anywhere] + [hbm] * 9,
        out_specs=hbm,
        scratch_shapes=like(*given)
        + [
            pltpu.VMEM((chunks * nvec, 2 * WIDE), BF16),
            pltpu.VMEM((leaves + 2, nvec, rank), F32),
            pltpu.VMEM((sources, PACK_ROWS, 2 * rank), F32),
            pltpu.VMEM((leaves + 2, 2, rank, 2 * rank), F32),
            pltpu.VMEM((nvec, rows_dev), F32),
            pltpu.VMEM((WIDE, 2 * WIDE), jnp.int16),
            pltpu.SMEM((2 * items,), jnp.int32),
            pltpu.SMEM((items,), jnp.int32),
            pltpu.SemaphoreType.DMA((11,)),
        ],
        compiler_params=params,
        name="far",
    )(
        sub_pos.astype(jnp.int32).reshape(1),
        leaf_src,
        leaf_count,
        node_src,
        node_count,
        *given,
    )


def solution(mesh):
    placed = (
        P(None, ("leaf", "grp")),
        P(None, ("leaf", "grp")),
        P(("leaf", "grp")),
        P(("leaf", "grp"), None, None),
        P(("leaf", "grp"), None, None),
        P(("leaf", "grp"), None, None),
        P(("leaf", "grp"), None, None),
        P(("leaf", "grp"), None, None),
        P("leaf", None, None),
        P(("leaf", "grp"), None),
        P(("leaf", "grp")),
        P(("leaf", "grp"), None),
        P(("leaf", "grp")),
    )
    return jax.shard_map(
        shards, mesh=mesh, in_specs=placed, out_specs=P(None, ("leaf", "grp")), check_vma=False
    )
```

profile of v0, /device:TPU:0, one launch (start us, length us, event | category | flops | bytes accessed | tf_op | source)
XLA Modules:
  0.0 65.4 jit_solution(9382211198255966963)
XLA Ops:
  0.0 9.9 %up.1 = (f32[16,16,512]{2,1,0:T(8,128)}, f32[8,24,128]{2,1,0:T(8,128)}, f32[32,24,128]{2,1,0:T(8,128)}) custom-call(f32[16,8192]{1,0:T(8,128)} %refs_0_.2, s32[64,128]{1,0:T(8,128)} %bitcast.3, f32[16,64,512]{2,1,0:T(8,128)} %refs_13_.1, f32[16,64,64]{2,1,0:T(8,128)} %refs_11_.1, f32[1,64,64]{2,1,0:T(8,128)} %refs_12_.1, f32[16,2,64]{2,1,0:T(2,128)} %refs_7_.3, ...), custom_call_target="tpu_custom_call" | custom-call | tf_op jit(solution)/shard_map/up/pallas_call | solution.py:482
  9.9 7.3 %all-to-all-start = ((f32[32,24,128]{2,1,0:T(8,128)}), f32[32,24,128]{2,1,0:T(8,128)S(1)}, u32[]{:S(2)}, u32[]{:S(2)}) async-start(f32[32,24,128]{2,1,0:T(8,128)} %get-tuple-element.11), calls=%async_computation | async-start | bytes 786432 | tf_op jit(solution)/shard_map/all_to_all | solution.py:501
  17.8 0.0 copy-start.1
  17.8 21.2 %near.1 = (f32[16,16,512]{2,1,0:T(8,128)}, s32[32,256]{1,0:T(8,128)}) custom-call(s32[1]{0:T(128)} %bitcast.2.shift, f32[2,8192]{1,0:T(2,128)} %refs_0_.3, s32[64,128]{1,0:T(8,128)} %bitcast.4, f32[16,16,512]{2,1,0:T(8,128)} %get-tuple-element.12.refs_2_), custom_call_target="tpu_custom_call" | custom-call | flops 536870912 | bytes 1048576 | tf_op jit(solution)/shard_map/near/pallas_call | solution.py:504
  39.1 0.0 copy-done.1
  39.1 7.2 %all_gather.3.refs_5_ = f32[32,24,128]{2,1,0:T(8,128)} all-gather(f32[8,24,128]{2,1,0:T(8,128)S(1)} %copy-done.1), channel_id=1, replica_groups=mesh['leaf'=8,'grp'=4] {'grp'}, dimensions={0}, use_global_device_ids=true | all-gather | bytes 491520 | tf_op jit(solution)/shard_map/all_gather | solution.py:502
  46.3 0.0 all-to-all-done.refs_6_
  46.3 0.0 copy-start
  46.3 0.7 %copy-done = f32[32,24,128]{2,1,0:T(8,128)} copy-done((f32[32,24,128]{2,1,0:T(8,128)}, f32[32,24,128]{2,1,0:T(8,128)S(1)}, u32[]{:S(2)}) %copy-start) | copy-done | bytes 393240
  47.0 18.4 %far.1 = f32[16,8192]{1,0:T(8,128)} custom-call(s32[1]{0:T(128)} %bitcast.refs_0_, s32[16,16]{1,0:T(8,128)} %refs_1_.1, s32[16]{0:T(128)} %refs_2_.3, s32[1,8]{1,0:T(1,128)} %refs_3_.3, s32[1]{0:T(128)S(6)} %copy.15.refs_4_, f32[32,24,128]{2,1,0:T(8,128)} %all_gather.3.refs_5_, f32[32,24,128]{2,1,0:T(8,128)} %copy-done, f32[16,2,64]{2,1,0:T(2,128)} %refs_7_.3, ...), custom_call_target="tpu_custom_call" | custom-call | tf_op jit(solution)/shard_map/far/pallas_call | solution.py:537
Async XLA Ops:
  9.9 36.4 %all-to-all-start = ((f32[32,24,128]{2,1,0:T(8,128)}), f32[32,24,128]{2,1,0:T(8,128)S(1)}, u32[]{:S(2)}, u32[]{:S(2)}) async-start(f32[32,24,128]{2,1,0:T(8,128)} %get-tuple-element.11), calls=%async_computation | async-start | bytes 786432 | tf_op jit(solution)/shard_map/all_to_all | solution.py:501
  17.8 21.3 %copy-start.1 = (f32[8,24,128]{2,1,0:T(8,128)S(1)}, f32[8,24,128]{2,1,0:T(8,128)}, u32[]{:S(2)}) copy-start(f32[8,24,128]{2,1,0:T(8,128)} %get-tuple-element.10) | copy-start | bytes 294916
  46.3 0.7 %copy-start = (f32[32,24,128]{2,1,0:T(8,128)}, f32[32,24,128]{2,1,0:T(8,128)S(1)}, u32[]{:S(2)}) copy-start(f32[32,24,128]{2,1,0:T(8,128)S(1)} %all-to-all-done.refs_6_) | copy-start | bytes 1179652
where the time goes:
time: 65.7 us; the launch traced here: 65.4 us
  Pallas kernels  49.5 us (75%)
  starting transfers between devices  7.29 us (11%)
  blocking collectives  7.18 us (11%)
  local copies, waits for them, and re-layouts  0.75 us (1%)
  between operations  0.71 us (1%)
    pallas_call x1, Pallas kernels, shards(): pl.pallas_call(near_kernel, out_shape=(jax.ShapeDtypeStruct((leaves, nvec...  21.2 us
    pallas_call x1, Pallas kernels, shards(): pl.pallas_call(functools.partial(far_kernel, groups, subtrees), out_shape...  18.4 us
    pallas_call x1, Pallas kernels, shards(): pl.pallas_call(up_kernel, out_shape=(jax.ShapeDtypeStruct((leaves, nvec,...  9.85 us
    all_to_all x1, starting transfers between devices, shards(): tree_all = lax.all_to_all(tree_pack, ('leaf', 'grp'), 0, 0, tiled=True)  7.29 us
    all_gather x1, blocking collectives, shards(): leaf_all = lax.all_gather(leaf_pack, 'grp', axis=0, tiled=True)  7.18 us
  transfers between devices with their start and end apart: 1, of which 0 were waited for; matrix products, arithmetic and copies ran while one was open for 0% of the time, Pallas kernels for 32%

commit v1 on v0

--- a/solution.py
+++ b/solution.py
@@ -16,7 +16,6 @@
 LOG2E = math.log2(math.e)
 TINY = 1e-37
 PACK_ROWS = 24
-PART = 32
 AT_ONCE = 4
 
 
@@ -161,14 +160,16 @@
 def near_kernel(shift, *refs):
     given, (near_out, inverse_out) = refs[:3], refs[3:5]
     held = refs[5:8]
-    near, inverse, flat, source, rows, across, down, slots, sems = refs[8:]
+    near, inverse, flat, source, rows, across, down, slots, order, sorts, sorted_vec = refs[8:19]
+    tables, marks_vmem, marks, sems = refs[19:]
     copies = fetch(list(zip(given, held)), sems)
     crd, perm, tree_vec = held
     count_rows(rows)
     leaves, nvec, block = tree_vec.shape
     chunks = crd.shape[1] // WIDE
     scale, poly = make_tables(1.0 / math.sqrt(block))
-    slope = scale[0, 1] - scale[0, 0]
+    slope = float(scale[0, 1] - scale[0, 0])
+    spread = np.concatenate([scale[None], poly], axis=0)
     copies[0].wait()
     for axis in range(2):
         for each in range(chunks):
@@ -181,8 +182,44 @@
         rest = rest - rounded.astype(F32)
     slots[...] = jnp.zeros_like(slots)
     copies[1].wait()
+
+    index = jnp.concatenate([leaf_index(perm, leaf, block) for leaf in range(leaves)], axis=0)
+    moved = index + shift[0]
+    kind = moved - 3 * ((moved * 43691) >> 17)
+    ones = [jnp.where(kind == each, 1.0, 0.0) for each in range(2)]
+    before = lax.broadcasted_iota(jnp.int32, (block, block), 0) < lax.broadcasted_iota(
+        jnp.int32, (block, block), 1
+    )
+    before = jnp.where(before, 1.0, 0.0).astype(BF16)
+    seen = dot(jnp.concatenate(ones, axis=0).astype(BF16), before)
+    seen_zero, seen_one = seen[:leaves], seen[leaves:]
+    size_zero, size_one = [jnp.sum(each, axis=1, keepdims=True) for each in ones]
+    lane = lax.broadcasted_iota(jnp.int32, (leaves, block), 1)
+    rank = jnp.where(
+        kind == 0,
+        seen_zero,
+        jnp.where(
+            kind == 1,
+            size_zero + seen_one,
+            size_zero + size_one + lane.astype(F32) - seen_zero - seen_one,
+        ),
+    )
+    order[...] = rank.astype(jnp.int32)
+    last = block // 8 - 1
+    border_zero = jnp.broadcast_to(size_zero.astype(jnp.int32), (leaves, 128))
+    border_one = jnp.broadcast_to((size_zero + size_one).astype(jnp.int32), (leaves, 128))
+    tile = lax.broadcasted_iota(jnp.int32, (leaves, 128), 1)
+    tile_zero = jnp.minimum(border_zero >> 3, last)
+    tile_one = jnp.minimum(border_one >> 3, last)
+    which = jnp.where(8 * tile >= border_zero, 1, 0) + jnp.where(8 * tile >= border_one, 1, 0)
+    which = jnp.where(tile == tile_zero, 3, jnp.where(tile == tile_one, 4, which))
+    which = jnp.where(tile == last + 1, border_zero, which)
+    which = jnp.where(tile == last + 2, border_one, which)
+    marks_vmem[...] = which
+    tell = pltpu.make_async_copy(marks_vmem, marks, sems.at[4])
+    tell.start()
+    copies[2].wait()
     side = 128
-    tiles = block // side
 
     def place_leaf(leaf, carry):
         index = leaf_index(perm, leaf, block)
@@ -195,76 +232,107 @@
         lane = lax.broadcasted_iota(jnp.int32, (chunks, block), 1) + leaf * block
         lane_low = (lane & (WIDE - 1)).astype(F32)
         lane_high = (lane >> SHIFT).astype(F32)
-        marks = jnp.concatenate(
+        own = jnp.concatenate(
             [jnp.where(mine, lane_low, 0.0), jnp.where(mine, lane_high, 0.0)], axis=0
         ).astype(BF16)
-        slots[...] += dot(marks, hot, True)
+        slots[...] += dot(own, hot, True)
         row_x = jnp.sum(jnp.where(mine, found[:chunks], 0.0), axis=0, keepdims=True)
         row_y = jnp.sum(jnp.where(mine, found[chunks:], 0.0), axis=0, keepdims=True)
-        moved = index + shift[0]
-        kind = moved - 3 * ((moved * 43691) >> 17)
-        row_w = kind.astype(F32) * slope
-        for place, row in enumerate((row_x, row_y, row_w)):
-            across[leaf, place] = jnp.broadcast_to(row, (8, block))
+        rest = jnp.concatenate([row_x, row_y, jnp.zeros((6, block), F32)], axis=0)
+        pieces = []
+        for piece in range(2):
+            rounded = rest.astype(BF16).astype(F32)
+            pieces.append(rounded)
+            rest = rest - rounded
+        pieces = jnp.concatenate(pieces + [rest, jnp.zeros((8, block), F32)], axis=0).astype(BF16)
+        vec_hi, vec_lo = parts(tree_vec[leaf])
+        place = order[pl.ds(leaf, 1), :]
+        sort = jnp.concatenate([one_hot(rows, place), one_hot(rows, place - WIDE)], axis=0)
+        sorts[leaf] = sort
+        moved = dot(jnp.concatenate([vec_hi, vec_lo, pieces], axis=0), sort, True)
+        sorted_vec[leaf] = moved[: 2 * nvec].astype(BF16)
+        moved = moved[2 * nvec :]
+        moved = moved[:8] + moved[8:16] + moved[16:24]
+        for axis in range(2):
+            row = moved[axis : axis + 1]
+            across[leaf, axis] = jnp.broadcast_to(row, (8, block))
             turned = jnp.transpose(jnp.broadcast_to(row, (side, block)))
-            down[leaf, place] = turned.reshape(block // 8, 8, side)
+            down[leaf, axis] = turned.reshape(block // 8, 8, side)
         return carry
 
     lax.fori_loop(0, leaves, place_leaf, 0, unroll=2)
     inverse[...] = (slots[:chunks] + slots[chunks:] * WIDE).astype(jnp.int32)
     leave = pltpu.make_async_copy(inverse, inverse_out, sems.at[3])
     leave.start()
-    copies[2].wait()
+    tell.wait()
 
     def one_leaf(leaf, carry):
-        vec_hi, vec_lo = parts(tree_vec[leaf])
-        vec_both = jnp.concatenate([vec_hi, vec_lo], axis=0)
-        total = [0.0] * tiles
-        for col in reversed(range(tiles)):
-            cols = slice(col * side, (col + 1) * side)
-            over_x, over_y, over_w = [across[leaf, each, :, cols] for each in range(3)]
-            over_zero, over_one = over_w > 0.5 * slope, over_w > 1.5 * slope
-
-            def across_table(power, first):
-                zero, one, two = [float(each) for each in poly[power, first]]
-                return jnp.where(over_zero, zero, jnp.where(over_one, one, two))[None]
-
-            table = [[across_table(power, first) for first in range(3)] for power in range(5)]
-            over_w = (over_w + float(scale[0, 0]))[None]
-            over_x, over_y = over_x[None], over_y[None]
+        border_zero, border_one = marks[leaf, last + 1], marks[leaf, last + 2]
+        lane = lax.broadcasted_iota(jnp.int32, (8, block), 1)
+        over_zero, over_one = lane < border_zero, lane < border_one
+        mixes = []
+        for border in (border_zero, border_one):
+            row = lax.broadcasted_iota(jnp.int32, (8, block), 0) + jnp.minimum(border >> 3, last) * 8
+            mixes.append((row < border_zero, row < border_one))
+        for power in range(6):
+            table = []
+            for first in range(3):
+                zero, one, two = [float(each) for each in spread[power, first]]
+                table.append(jnp.where(over_zero, zero, jnp.where(over_one, one, two)))
+                tables[first, power] = table[first]
+            for each, (row_zero, row_one) in enumerate(mixes):
+                tables[3 + each, power] = jnp.where(
+                    row_zero, table[0], jnp.where(row_one, table[1], table[2])
+                )
+        vec_both = sorted_vec[leaf]
+        vec_hi = vec_both[:nvec]
+        total = [0.0] * (block // side)
+
+        def add(first, terms):
+            for each in range(terms.shape[1] // side):
+                total[first + each] = total[first + each] + terms[:, each * side : (each + 1) * side]
+
+        def apply(cols, high, low, turned):
+            both = dot(vec_both[:, cols], high, turned)
+            return both[:nvec] + both[nvec:] + dot(vec_hi[:, cols], low, turned)
+
+        for pair in reversed(range(block // WIDE)):
+            at = [slice((2 * pair + each) * side, (2 * pair + each + 1) * side) for each in range(2)]
+            over = [[across[leaf, axis, :, cols] for axis in range(2)] for cols in at]
             high, low = [], []
-            for row in range((col + 1) * side // PART):
-                at = slice(row * PART // 8, (row + 1) * PART // 8)
-                diff_x = down[leaf, 0, at] - over_x
-                diff_y = down[leaf, 1, at] - over_y
-                down_w = down[leaf, 2, at]
-                var_zero, var_one = down_w > 0.5 * slope, down_w > 1.5 * slope
-                square = (diff_x * diff_x + diff_y * diff_y) * (down_w + over_w)
-                arg = square * lax.rsqrt(TINY - square)
-                value = jnp.where(var_one, 0.0, table[4][2])
-                value = value * arg + jnp.where(
-                    var_zero, 0.0, jnp.where(var_one, table[3][1], table[3][2])
-                )
-                for power in (2, 1, 0):
-                    a, b, c = table[power]
-                    value = value * arg + jnp.where(var_zero, a, jnp.where(var_one, b, c))
-                value = (value * jnp.exp2(arg)).reshape(PART, side)
-                value_hi, value_lo = parts(value)
+            for step in range((pair + 1) * WIDE // 16):
+                halves = []
+                for half in range(2):
+                    if half == 0 and step * 16 >= pair * WIDE + side:
+                        halves.append(jnp.zeros((16, side), F32))
+                        continue
+                    values = []
+                    for each in (2 * step, 2 * step + 1):
+                        which = marks[leaf, each]
+                        diff_x = down[leaf, 0, each] - over[half][0]
+                        diff_y = down[leaf, 1, each] - over[half][1]
+                        square = (diff_x * diff_x + diff_y * diff_y) * tables[which, 0, :, at[half]]
+                        arg = square * lax.rsqrt(TINY - square)
+                        value = tables[which, 5, :, at[half]]
+                        for power in (4, 3, 2, 1):
+                            value = value * arg + tables[which, power, :, at[half]]
+                        values.append(value * jnp.exp2(arg))
+                    halves.append(jnp.concatenate(values, axis=0))
+                value_hi, value_lo = parts(jnp.concatenate(halves, axis=1))
                 high.append(value_hi)
                 low.append(value_lo)
             high = jnp.concatenate(high, axis=0)
             low = jnp.concatenate(low, axis=0)
-            upto = (col + 1) * side
-            both = dot(vec_both[:, :upto], high)
-            direct = both[:nvec] + both[nvec:] + dot(vec_hi[:, :upto], low)
-            total[col] = total[col] + direct
-            if col > 0:
-                both = dot(vec_both[:, cols], high[: col * side], True)
-                back = both[:nvec] + both[nvec:] + dot(vec_hi[:, cols], low[: col * side], True)
-                for row in range(col):
-                    total[row] = total[row] + back[:, row * side : (row + 1) * side]
-        for col in range(tiles):
-            near[leaf, :, col * side : (col + 1) * side] = total[col]
+            start = pair * WIDE
+            add(2 * pair, apply(slice(0, start + WIDE), high, low, False))
+            if pair > 0:
+                add(0, apply(slice(start, start + WIDE), high[:start], low[:start], True))
+            corner = slice(start, start + side)
+            add(2 * pair, apply(at[1], high[corner, side:], low[corner, side:], True))
+        whole = jnp.concatenate(total, axis=1)
+        whole_hi, whole_lo = parts(whole)
+        both = dot(jnp.concatenate([whole_hi, whole_lo], axis=0), sorts[leaf])
+        near[leaf] = both[:nvec] + both[nvec:]
         return carry
 
     lax.fori_loop(0, leaves, one_leaf, 0)
@@ -516,10 +584,16 @@
             pltpu.VMEM((2 * chunks, WIDE), F32),
             pltpu.VMEM((6 * chunks, WIDE), BF16),
             pltpu.VMEM((WIDE, block), jnp.int16),
-            pltpu.VMEM((leaves, 3, 8, block), F32),
-            pltpu.VMEM((leaves, 3, block // 8, 8, 128), F32),
+            pltpu.VMEM((leaves, 2, 8, block), F32),
+            pltpu.VMEM((leaves, 2, block // 8, 8, 128), F32),
             pltpu.VMEM((2 * chunks, WIDE), F32),
-            pltpu.SemaphoreType.DMA((4,)),
+            pltpu.VMEM((leaves, block), jnp.int32),
+            pltpu.VMEM((leaves, block, block), BF16),
+            pltpu.VMEM((leaves, 2 * nvec, block), BF16),
+            pltpu.VMEM((5, 6, 8, block), F32),
+            pltpu.VMEM((leaves, 128), jnp.int32),
+            pltpu.SMEM((leaves, 128), jnp.int32),
+            pltpu.SemaphoreType.DMA((5,)),
         ],
         compiler_params=params,
         cost_estimate=pl.CostEstimate(

time: 65.7 us -> 67.1 us (1.021)
  the two profiles are of different devices: /device:TPU:0 before, /device:TPU:5 now
where the time goes in v1:
time: 67.1 us; the launch traced here: 65.9 us
  Pallas kernels  51 us (76%)
  blocking collectives  7.03 us (10%)
  starting transfers between devices  6.42 us (10%)
  local copies, waits for them, and re-layouts  0.75 us (1%)
  between operations  0.71 us (1%)
    pallas_call x1, Pallas kernels, shards(): pl.pallas_call(near_kernel, out_shape=(jax.ShapeDtypeStruct((leaves, nvec...  23.3 us
    pallas_call x1, Pallas kernels, shards(): pl.pallas_call(functools.partial(far_kernel, groups, subtrees), out_shape...  17.8 us
    pallas_call x1, Pallas kernels, shards(): pl.pallas_call(up_kernel, out_shape=(jax.ShapeDtypeStruct((leaves, nvec,...  9.85 us
    all_gather x1, blocking collectives, shards(): leaf_all = lax.all_gather(leaf_pack, 'grp', axis=0, tiled=True)  7.03 us
    all_to_all x1, starting transfers between devices, shards(): tree_all = lax.all_to_all(tree_pack, ('leaf', 'grp'), 0, 0, tiled=True)  6.42 us
  transfers between devices with their start and end apart: 1, of which 0 were waited for; matrix products, arithmetic and copies ran while one was open for 0% of the time, Pallas kernels for 35%

profile of v1, /device:TPU:5, one launch (start us, length us, event | category | flops | bytes accessed | tf_op | source)
XLA Modules:
  0.0 65.9 jit_solution(18202135599202648662)
XLA Ops:
  0.0 9.8 %up.1 = (f32[16,16,512]{2,1,0:T(8,128)}, f32[8,24,128]{2,1,0:T(8,128)}, f32[32,24,128]{2,1,0:T(8,128)}) custom-call(f32[16,8192]{1,0:T(8,128)} %refs_0_.2, s32[64,128]{1,0:T(8,128)} %bitcast.3, f32[16,64,512]{2,1,0:T(8,128)} %refs_13_.1, f32[16,64,64]{2,1,0:T(8,128)} %refs_11_.1, f32[1,64,64]{2,1,0:T(8,128)} %refs_12_.1, f32[16,2,64]{2,1,0:T(2,128)} %refs_7_.3, ...), custom_call_target="tpu_custom_call" | custom-call | tf_op jit(solution)/shard_map/up/pallas_call | solution.py:550
  9.9 6.4 %all-to-all-start = ((f32[32,24,128]{2,1,0:T(8,128)}), f32[32,24,128]{2,1,0:T(8,128)S(1)}, u32[]{:S(2)}, u32[]{:S(2)}) async-start(f32[32,24,128]{2,1,0:T(8,128)} %get-tuple-element.11), calls=%async_computation | async-start | bytes 786432 | tf_op jit(solution)/shard_map/all_to_all | solution.py:569
  16.9 0.0 copy-start.1
  17.0 23.3 %near.1 = (f32[16,16,512]{2,1,0:T(8,128)}, s32[32,256]{1,0:T(8,128)}) custom-call(s32[1]{0:T(128)} %bitcast.2.shift, f32[2,8192]{1,0:T(2,128)} %refs_0_.3, s32[64,128]{1,0:T(8,128)} %bitcast.4, f32[16,16,512]{2,1,0:T(8,128)} %get-tuple-element.12.refs_2_), custom_call_target="tpu_custom_call" | custom-call | flops 536870912 | bytes 1048576 | tf_op jit(solution)/shard_map/near/pallas_call | solution.py:572
  40.2 0.0 copy-done.1
  40.2 7.0 %all_gather.3.refs_5_ = f32[32,24,128]{2,1,0:T(8,128)} all-gather(f32[8,24,128]{2,1,0:T(8,128)S(1)} %copy-done.1), channel_id=1, replica_groups=mesh['leaf'=8,'grp'=4] {'grp'}, dimensions={0}, use_global_device_ids=true | all-gather | bytes 491520 | tf_op jit(solution)/shard_map/all_gather | solution.py:570
  47.3 0.0 all-to-all-done.refs_6_
  47.3 0.0 copy-start
  47.3 0.7 %copy-done = f32[32,24,128]{2,1,0:T(8,128)} copy-done((f32[32,24,128]{2,1,0:T(8,128)}, f32[32,24,128]{2,1,0:T(8,128)S(1)}, u32[]{:S(2)}) %copy-start) | copy-done | bytes 393240
  48.0 17.8 %far.1 = f32[16,8192]{1,0:T(8,128)} custom-call(s32[1]{0:T(128)} %bitcast.refs_0_, s32[16,16]{1,0:T(8,128)} %refs_1_.1, s32[16]{0:T(128)} %refs_2_.3, s32[1,8]{1,0:T(1,128)} %refs_3_.3, s32[1]{0:T(128)S(6)} %copy.15.refs_4_, f32[32,24,128]{2,1,0:T(8,128)} %all_gather.3.refs_5_, f32[32,24,128]{2,1,0:T(8,128)} %copy-done, f32[16,2,64]{2,1,0:T(2,128)} %refs_7_.3, ...), custom_call_target="tpu_custom_call" | custom-call | tf_op jit(solution)/shard_map/far/pallas_call | solution.py:611
Async XLA Ops:
  9.9 37.4 %all-to-all-start = ((f32[32,24,128]{2,1,0:T(8,128)}), f32[32,24,128]{2,1,0:T(8,128)S(1)}, u32[]{:S(2)}, u32[]{:S(2)}) async-start(f32[32,24,128]{2,1,0:T(8,128)} %get-tuple-element.11), calls=%async_computation | async-start | bytes 786432 | tf_op jit(solution)/shard_map/all_to_all | solution.py:569
  16.9 23.3 %copy-start.1 = (f32[8,24,128]{2,1,0:T(8,128)S(1)}, f32[8,24,128]{2,1,0:T(8,128)}, u32[]{:S(2)}) copy-start(f32[8,24,128]{2,1,0:T(8,128)} %get-tuple-element.10) | copy-start | bytes 294916
  47.3 0.7 %copy-start = (f32[32,24,128]{2,1,0:T(8,128)}, f32[32,24,128]{2,1,0:T(8,128)S(1)}, u32[]{:S(2)}) copy-start(f32[32,24,128]{2,1,0:T(8,128)S(1)} %all-to-all-done.refs_6_) | copy-start | bytes 1179652

commit v2 on v0

--- a/solution.py
+++ b/solution.py
@@ -11,8 +11,8 @@
 
 F32 = jnp.float32
 BF16 = jnp.bfloat16
-WIDE = 256
-SHIFT = 8
+WIDE = 128
+SHIFT = 7
 LOG2E = math.log2(math.e)
 TINY = 1e-37
 PACK_ROWS = 24
@@ -161,7 +161,8 @@
 def near_kernel(shift, *refs):
     given, (near_out, inverse_out) = refs[:3], refs[3:5]
     held = refs[5:8]
-    near, inverse, flat, source, rows, across, down, slots, sems = refs[8:]
+    near, inverse, flat, source, rows, across, down, slots = refs[8:16]
+    sooner, later, sems = refs[16:18], refs[18:20], refs[20]
     copies = fetch(list(zip(given, held)), sems)
     crd, perm, tree_vec = held
     count_rows(rows)
@@ -216,11 +217,8 @@
     leave.start()
     copies[2].wait()
 
-    def one_leaf(leaf, carry):
-        vec_hi, vec_lo = parts(tree_vec[leaf])
-        vec_both = jnp.concatenate([vec_hi, vec_lo], axis=0)
-        total = [0.0] * tiles
-        for col in reversed(range(tiles)):
+    def values(leaf, high, low):
+        for col in range(tiles):
             cols = slice(col * side, (col + 1) * side)
             over_x, over_y, over_w = [across[leaf, each, :, cols] for each in range(3)]
             over_zero, over_one = over_w > 0.5 * slope, over_w > 1.5 * slope
@@ -232,42 +230,49 @@
             table = [[across_table(power, first) for first in range(3)] for power in range(5)]
             over_w = (over_w + float(scale[0, 0]))[None]
             over_x, over_y = over_x[None], over_y[None]
-            high, low = [], []
-            for row in range((col + 1) * side // PART):
-                at = slice(row * PART // 8, (row + 1) * PART // 8)
-                diff_x = down[leaf, 0, at] - over_x
-                diff_y = down[leaf, 1, at] - over_y
-                down_w = down[leaf, 2, at]
-                var_zero, var_one = down_w > 0.5 * slope, down_w > 1.5 * slope
-                square = (diff_x * diff_x + diff_y * diff_y) * (down_w + over_w)
-                arg = square * lax.rsqrt(TINY - square)
-                value = jnp.where(var_one, 0.0, table[4][2])
-                value = value * arg + jnp.where(
-                    var_zero, 0.0, jnp.where(var_one, table[3][1], table[3][2])
-                )
-                for power in (2, 1, 0):
-                    a, b, c = table[power]
-                    value = value * arg + jnp.where(var_zero, a, jnp.where(var_one, b, c))
-                value = (value * jnp.exp2(arg)).reshape(PART, side)
-                value_hi, value_lo = parts(value)
-                high.append(value_hi)
-                low.append(value_lo)
-            high = jnp.concatenate(high, axis=0)
-            low = jnp.concatenate(low, axis=0)
-            upto = (col + 1) * side
-            both = dot(vec_both[:, :upto], high)
-            direct = both[:nvec] + both[nvec:] + dot(vec_hi[:, :upto], low)
-            total[col] = total[col] + direct
-            if col > 0:
-                both = dot(vec_both[:, cols], high[: col * side], True)
-                back = both[:nvec] + both[nvec:] + dot(vec_hi[:, cols], low[: col * side], True)
-                for row in range(col):
-                    total[row] = total[row] + back[:, row * side : (row + 1) * side]
-        for col in range(tiles):
-            near[leaf, :, col * side : (col + 1) * side] = total[col]
-        return carry
-
-    lax.fori_loop(0, leaves, one_leaf, 0)
+            for row in range(col + 1):
+                pieces = []
+                for part in range(side // PART):
+                    first = row * side + part * PART
+                    at = slice(first // 8, (first + PART) // 8)
+                    diff_x = down[leaf, 0, at] - over_x
+                    diff_y = down[leaf, 1, at] - over_y
+                    down_w = down[leaf, 2, at]
+                    var_zero, var_one = down_w > 0.5 * slope, down_w > 1.5 * slope
+                    square = (diff_x * diff_x + diff_y * diff_y) * (down_w + over_w)
+                    arg = square * lax.rsqrt(TINY - square)
+                    value = jnp.where(var_one, 0.0, table[4][2])
+                    value = value * arg + jnp.where(
+                        var_zero, 0.0, jnp.where(var_one, table[3][1], table[3][2])
+                    )
+                    for power in (2, 1, 0):
+                        a, b, c = table[power]
+                        value = value * arg + jnp.where(var_zero, a, jnp.where(var_one, b, c))
+                    pieces.append(parts((value * jnp.exp2(arg)).reshape(PART, side)))
+                rows = slice(row * side, (row + 1) * side)
+                for each, out in enumerate((high, low)):
+                    tile = jnp.concatenate([piece[each] for piece in pieces], axis=0)
+                    out[rows, cols] = tile
+                    if row < col:
+                        out[cols, rows] = jnp.transpose(tile)
+
+    def apply(leaf, high, low):
+        vec_hi, vec_lo = parts(tree_vec[leaf])
+        both = dot(jnp.concatenate([vec_hi, vec_lo], axis=0), high[...])
+        near[leaf] = both[:nvec] + both[nvec:] + dot(vec_hi, low[...])
+
+    for each in later:
+        each[...] = jnp.zeros_like(each)
+
+    def two_leaves(step, carry):
+        apply(jnp.maximum(2 * step - 1, 0), *later)
+        values(2 * step, *sooner)
+        apply(2 * step, *sooner)
+        values(2 * step + 1, *later)
+        return carry
+
+    lax.fori_loop(0, leaves // 2, two_leaves, 0)
+    apply(leaves - 1, *later)
     leave.wait()
     leave = pltpu.make_async_copy(near, near_out, sems.at[3])
     leave.start()
@@ -416,20 +421,17 @@
             )
 
     def scatter(each, carry):
-        at = pl.multiple_of(each * 2 * WIDE, 2 * WIDE)
-        index = jnp.concatenate(
-            [inverse[pl.ds(2 * each, 1), :], inverse[pl.ds(2 * each + 1, 1), :]], axis=1
-        )
-        out[:, pl.ds(at, 2 * WIDE)] = pick(rows, source, index, nvec)
-        return carry
-
-    steps = inverse.shape[0] // 2
+        at = pl.multiple_of(each * block, block)
+        out[:, pl.ds(at, block)] = pick(rows, source, leaf_index(inverse, each, block), nvec)
+        return carry
+
+    steps = inverse.shape[0] * WIDE // block
     segments = 4
     leaving = []
     for each in range(segments):
         start, stop = each * steps // segments, (each + 1) * steps // segments
         lax.fori_loop(start, stop, scatter, 0, unroll=2)
-        span = slice(start * 2 * WIDE, stop * 2 * WIDE)
+        span = slice(start * block, stop * block)
         leaving.append(pltpu.make_async_copy(out.at[:, span], out_at.at[:, span], sems.at[each]))
         leaving[-1].start()
     for copy in leaving:
@@ -519,6 +521,7 @@
             pltpu.VMEM((leaves, 3, 8, block), F32),
             pltpu.VMEM((leaves, 3, block // 8, 8, 128), F32),
             pltpu.VMEM((2 * chunks, WIDE), F32),
+            *[pltpu.VMEM((block, block), BF16)] * 4,
             pltpu.SemaphoreType.DMA((4,)),
         ],
         compiler_params=params,
@@ -546,7 +549,7 @@
             pltpu.VMEM((sources, PACK_ROWS, 2 * rank), F32),
             pltpu.VMEM((leaves + 2, 2, rank, 2 * rank), F32),
             pltpu.VMEM((nvec, rows_dev), F32),
-            pltpu.VMEM((WIDE, 2 * WIDE), jnp.int16),
+            pltpu.VMEM((WIDE, block), jnp.int16),
             pltpu.SMEM((2 * items,), jnp.int32),
             pltpu.SMEM((items,), jnp.int32),
             pltpu.SemaphoreType.DMA((11,)),

time: 65.7 us -> 65.1 us (level)
  the two profiles are of different devices: /device:TPU:0 before, /device:TPU:25 now
where the time goes in v2:
time: 65.1 us; the launch traced here: 64.8 us
  Pallas kernels  50 us (77%)
  blocking collectives  7.11 us (11%)
  starting transfers between devices  6.19 us (10%)
  local copies, waits for them, and re-layouts  0.75 us (1%)
  between operations  0.71 us (1%)
    pallas_call x1, Pallas kernels, shards(): pl.pallas_call(near_kernel, out_shape=(jax.ShapeDtypeStruct((leaves, nvec...  21.5 us
    pallas_call x1, Pallas kernels, shards(): pl.pallas_call(functools.partial(far_kernel, groups, subtrees), out_shape...  18.6 us
    pallas_call x1, Pallas kernels, shards(): pl.pallas_call(up_kernel, out_shape=(jax.ShapeDtypeStruct((leaves, nvec,...  9.85 us
    all_gather x1, blocking collectives, shards(): leaf_all = lax.all_gather(leaf_pack, 'grp', axis=0, tiled=True)  7.11 us
    all_to_all x1, starting transfers between devices, shards(): tree_all = lax.all_to_all(tree_pack, ('leaf', 'grp'), 0, 0, tiled=True)  6.19 us
  transfers between devices with their start and end apart: 1, of which 0 were waited for; matrix products, arithmetic and copies ran while one was open for 0% of the time, Pallas kernels for 33%

profile of v2, /device:TPU:25, one launch (start us, length us, event | category | flops | bytes accessed | tf_op | source)
XLA Modules:
  0.0 64.8 jit_solution(5078149622279971426)
XLA Ops:
  0.0 9.9 %up.1 = (f32[16,16,512]{2,1,0:T(8,128)}, f32[8,24,128]{2,1,0:T(8,128)}, f32[32,24,128]{2,1,0:T(8,128)}) custom-call(f32[16,8192]{1,0:T(8,128)} %refs_0_.2, s32[64,128]{1,0:T(8,128)} %bitcast.3, f32[16,64,512]{2,1,0:T(8,128)} %refs_13_.1, f32[16,64,64]{2,1,0:T(8,128)} %refs_11_.1, f32[1,64,64]{2,1,0:T(8,128)} %refs_12_.1, f32[16,2,64]{2,1,0:T(2,128)} %refs_7_.3, ...), custom_call_target="tpu_custom_call" | custom-call | tf_op jit(solution)/shard_map/up/pallas_call | solution.py:484
  9.9 6.2 %all-to-all-start = ((f32[32,24,128]{2,1,0:T(8,128)}), f32[32,24,128]{2,1,0:T(8,128)S(1)}, u32[]{:S(2)}, u32[]{:S(2)}) async-start(f32[32,24,128]{2,1,0:T(8,128)} %get-tuple-element.11), calls=%async_computation | async-start | bytes 786432 | tf_op jit(solution)/shard_map/all_to_all | solution.py:503
  16.7 0.0 copy-start.1
  16.7 21.5 %near.1 = (f32[16,16,512]{2,1,0:T(8,128)}, s32[64,128]{1,0:T(8,128)}) custom-call(s32[1]{0:T(128)} %bitcast.2.shift, f32[2,8192]{1,0:T(2,128)} %refs_0_.3, s32[64,128]{1,0:T(8,128)} %bitcast.4, f32[16,16,512]{2,1,0:T(8,128)} %get-tuple-element.12.refs_2_), custom_call_target="tpu_custom_call" | custom-call | flops 536870912 | bytes 1048576 | tf_op jit(solution)/shard_map/near/pallas_call | solution.py:506
  38.3 0.0 copy-done.1
  38.3 7.1 %all_gather.3.refs_5_ = f32[32,24,128]{2,1,0:T(8,128)} all-gather(f32[8,24,128]{2,1,0:T(8,128)S(1)} %copy-done.1), channel_id=1, replica_groups=mesh['leaf'=8,'grp'=4] {'grp'}, dimensions={0}, use_global_device_ids=true | all-gather | bytes 491520 | tf_op jit(solution)/shard_map/all_gather | solution.py:504
  45.4 0.0 all-to-all-done.refs_6_
  45.4 0.0 copy-start
  45.4 0.7 %copy-done = f32[32,24,128]{2,1,0:T(8,128)} copy-done((f32[32,24,128]{2,1,0:T(8,128)}, f32[32,24,128]{2,1,0:T(8,128)S(1)}, u32[]{:S(2)}) %copy-start) | copy-done | bytes 393240
  46.1 18.6 %far.1 = f32[16,8192]{1,0:T(8,128)} custom-call(s32[1]{0:T(128)} %bitcast.refs_0_, s32[16,16]{1,0:T(8,128)} %refs_1_.1, s32[16]{0:T(128)} %refs_2_.3, s32[1,8]{1,0:T(1,128)} %refs_3_.3, s32[1]{0:T(128)S(6)} %copy.15.refs_4_, f32[32,24,128]{2,1,0:T(8,128)} %all_gather.3.refs_5_, f32[32,24,128]{2,1,0:T(8,128)} %copy-done, f32[16,2,64]{2,1,0:T(2,128)} %refs_7_.3, ...), custom_call_target="tpu_custom_call" | custom-call | tf_op jit(solution)/shard_map/far/pallas_call | solution.py:540
Async XLA Ops:
  9.9 35.5 %all-to-all-start = ((f32[32,24,128]{2,1,0:T(8,128)}), f32[32,24,128]{2,1,0:T(8,128)S(1)}, u32[]{:S(2)}, u32[]{:S(2)}) async-start(f32[32,24,128]{2,1,0:T(8,128)} %get-tuple-element.11), calls=%async_computation | async-start | bytes 786432 | tf_op jit(solution)/shard_map/all_to_all | solution.py:503
  16.7 21.5 %copy-start.1 = (f32[8,24,128]{2,1,0:T(8,128)S(1)}, f32[8,24,128]{2,1,0:T(8,128)}, u32[]{:S(2)}) copy-start(f32[8,24,128]{2,1,0:T(8,128)} %get-tuple-element.10) | copy-start | bytes 294916
  45.4 0.7 %copy-start = (f32[32,24,128]{2,1,0:T(8,128)}, f32[32,24,128]{2,1,0:T(8,128)S(1)}, u32[]{:S(2)}) copy-start(f32[32,24,128]{2,1,0:T(8,128)S(1)} %all-to-all-done.refs_6_) | copy-start | bytes 1179652

commit v3 on v2

--- a/solution.py
+++ b/solution.py
@@ -3,6 +3,7 @@
 
 import jax
 import jax.numpy as jnp
+import ml_dtypes
 import numpy as np
 from jax import lax
 from jax.experimental import pallas as pl
@@ -185,6 +186,23 @@
     side = 128
     tiles = block // side
 
+    def three(row):
+        pieces = []
+        for _ in range(3):
+            pieces.append(row.astype(BF16).astype(F32))
+            row = row - pieces[-1]
+        return pieces
+
+    part = lax.broadcasted_iota(jnp.int32, (16, 3 * side), 0)
+    third = lax.broadcasted_iota(jnp.int32, (16, 3 * side), 1) // side
+    widen = jnp.where((part < 6) & (part // 3 == third), 1.0, 0.0)
+    left = np.float32(slope)
+    for each in range(3):
+        piece = np.float32(left.astype(ml_dtypes.bfloat16))
+        widen = jnp.where((part == 6 + each) & (third == 2), float(piece), widen)
+        left = left - piece
+    widen = widen.astype(BF16)
+
     def place_leaf(leaf, carry):
         index = leaf_index(perm, leaf, block)
         hot = one_hot(rows, index & (WIDE - 1))
@@ -207,11 +225,15 @@
         row_w = kind.astype(F32) * slope
         for place, row in enumerate((row_x, row_y, row_w)):
             across[leaf, place] = jnp.broadcast_to(row, (8, block))
-            turned = jnp.transpose(jnp.broadcast_to(row, (side, block)))
-            down[leaf, place] = turned.reshape(block // 8, 8, side)
-        return carry
-
-    lax.fori_loop(0, leaves, place_leaf, 0, unroll=2)
+        stack = three(row_x) + three(row_y) + [kind.astype(F32)] * 3
+        stack = jnp.concatenate(stack + [jnp.zeros((7, block), F32)], axis=0).astype(BF16)
+        columns = dot(jnp.transpose(stack), widen)
+        for place in range(3):
+            column = columns[:, place * side : (place + 1) * side]
+            down[leaf, place] = column.reshape(block // 8, 8, side)
+        return carry
+
+    lax.fori_loop(0, leaves, place_leaf, 0, unroll=4)
     inverse[...] = (slots[:chunks] + slots[chunks:] * WIDE).astype(jnp.int32)
     leave = pltpu.make_async_copy(inverse, inverse_out, sems.at[3])
     leave.start()
@@ -271,22 +293,31 @@
         values(2 * step + 1, *later)
         return carry
 
-    lax.fori_loop(0, leaves // 2, two_leaves, 0)
+    lax.fori_loop(0, leaves // 4, two_leaves, 0)
+    half = slice(0, leaves // 2 - 1)
+    first = pltpu.make_async_copy(near.at[half], near_out.at[half], sems.at[0])
+    first.start()
+    lax.fori_loop(leaves // 4, leaves // 2, two_leaves, 0)
     apply(leaves - 1, *later)
-    leave.wait()
-    leave = pltpu.make_async_copy(near, near_out, sems.at[3])
-    leave.start()
-    leave.wait()
+    half = slice(leaves // 2 - 1, leaves)
+    second = pltpu.make_async_copy(near.at[half], near_out.at[half], sems.at[1])
+    second.start()
+    for copy in (leave, first, second):
+        copy.wait()
 
 
 def far_kernel(groups, subtrees, *refs):
     place, leaf_src, leaf_count, node_src, node_count = refs[:5]
-    given, out_at = refs[5:16], refs[16]
-    held = refs[17:28]
-    source, coef, twice, cols, out, rows, srcs, dsts, sems = refs[28:]
-    copies = fetch(list(zip(given, held)), sems)
-    leaf_all, tree_all, leaf_skel, node_skel, sub_skel, tables = held[:6]
-    leaf_maps, node_maps, bases, near, inverse = held[6:]
+    leaf_packs, refs = refs[5 : 5 + groups], refs[5 + groups :]
+    given, out_at, held = refs[:10], refs[10], refs[11:21]
+    leaf_all, source, coef, twice, cols, out, rows, srcs, dsts, sems = refs[21:]
+    own = leaf_packs[0].shape[0]
+    owner = [lax.rem(place[1] - shift + groups, groups) for shift in range(groups)]
+    arrive = [leaf_all.at[pl.ds(each * own, own)] for each in owner]
+    copies = fetch(list(zip(leaf_packs + given, arrive + list(held))), sems)
+    leaf_copies, copies = copies[:groups], [None] + copies[groups:]
+    tree_all, leaf_skel, node_skel, sub_skel, tables = held[:5]
+    leaf_maps, node_maps, bases, near, inverse = held[5:]
     count_rows(rows)
     leaves, nvec, block = near.shape
     rank = bases.shape[1]
@@ -340,7 +371,8 @@
         srcs[2 * (ends + each) + 1] = blank
         dsts[ends + each] = leaves + 1
 
-    copies[0].wait()
+    for copy in leaf_copies:
+        copy.wait()
 
     def both_leaves(pair, carry):
         packs = leaf_all[pair]
@@ -501,7 +533,10 @@
         name="up",
     )(*given)
     tree_all = lax.all_to_all(tree_pack, ("leaf", "grp"), 0, 0, tiled=True)
-    leaf_all = lax.all_gather(leaf_pack, "grp", axis=0, tiled=True)
+    leaf_all = [leaf_pack] + [
+        lax.ppermute(leaf_pack, "grp", [(each, (each + shift) % groups) for each in range(groups)])
+        for shift in range(1, groups)
+    ]
     shift = (device_pos * (rows_dev % 3) % 3).astype(jnp.int32).reshape(1)
     near, inverse = pl.pallas_call(
         near_kernel,
@@ -533,17 +568,18 @@
         name="near",
     )(shift, coords, order, tree_vec)
     tables = jnp.asarray(skeleton_tables(rank))
-    given = (leaf_all, tree_all, leaf_skel, node_skel, sub_skel, tables)
+    given = (tree_all, leaf_skel, node_skel, sub_skel, tables)
     given = given + (leaf_maps, node_maps, bases, near, inverse)
     items = (leaf_src.size + node_src.size + subtrees + 2) // 2 + AT_ONCE
     sources = groups * leaves + 3 * groups + subtrees + 1
     return pl.pallas_call(
         functools.partial(far_kernel, groups, subtrees),
         out_shape=jax.ShapeDtypeStruct((nvec, rows_dev), F32),
-        in_specs=[smem] * 5 + [hbm, anywhere] + [hbm] * 9,
+        in_specs=[smem] * 5 + [anywhere] * (groups + 1) + [hbm] * 9,
         out_specs=hbm,
         scratch_shapes=like(*given)
         + [
+            pltpu.VMEM((groups * leaf_pack.shape[0],) + leaf_pack.shape[1:], F32),
             pltpu.VMEM((chunks * nvec, 2 * WIDE), BF16),
             pltpu.VMEM((leaves + 2, nvec, rank), F32),
             pltpu.VMEM((sources, PACK_ROWS, 2 * rank), F32),
@@ -552,16 +588,17 @@
             pltpu.VMEM((WIDE, block), jnp.int16),
             pltpu.SMEM((2 * items,), jnp.int32),
             pltpu.SMEM((items,), jnp.int32),
-            pltpu.SemaphoreType.DMA((11,)),
+            pltpu.SemaphoreType.DMA((10 + groups,)),
         ],
         compiler_params=params,
         name="far",
     )(
-        sub_pos.astype(jnp.int32).reshape(1),
+        jnp.stack([sub_pos, lax.axis_index("grp")]).astype(jnp.int32),
         leaf_src,
         leaf_count,
         node_src,
         node_count,
+        *leaf_all,
         *given,
     )
 

time: 65.1 us -> 63.9 us (0.982)
  the two profiles are of different devices: /device:TPU:25 before, /device:TPU:0 now
where the time goes in v3:
time: 63.9 us; the launch traced here: 63.6 us
  Pallas kernels  50.8 us (79%)
  starting transfers between devices  10.6 us (17%)
  local copies, waits for them, and re-layouts  0.83 us (1%)
  between operations  0.73 us (1%)
    pallas_call x1, Pallas kernels, shards(): pl.pallas_call(near_kernel, out_shape=(jax.ShapeDtypeStruct((leaves, nvec...  23.4 us
    pallas_call x1, Pallas kernels, shards(): pl.pallas_call(functools.partial(far_kernel, groups, subtrees), out_shape...  17.5 us
    pallas_call x1, Pallas kernels, shards(): pl.pallas_call(up_kernel, out_shape=(jax.ShapeDtypeStruct((leaves, nvec,...  9.86 us
    all_to_all x1, starting transfers between devices, shards(): tree_all = lax.all_to_all(tree_pack, ('leaf', 'grp'), 0, 0, tiled=True)  7.3 us
    ppermute x3, starting transfers between devices, shards(): lax.ppermute(leaf_pack, 'grp', [(each, (each + shift) % groups) for each...  3.3 us
  transfers between devices with their start and end apart: 4, of which 0 were waited for; matrix products, arithmetic and copies ran while one was open for 1% of the time, Pallas kernels for 37%

profile of v3, /device:TPU:0, one launch (start us, length us, event | category | flops | bytes accessed | tf_op | source)
XLA Modules:
  0.0 63.6 jit_solution(8311914933147602859)
XLA Ops:
  0.0 9.9 %up.1 = (f32[16,16,512]{2,1,0:T(8,128)}, f32[8,24,128]{2,1,0:T(8,128)}, f32[32,24,128]{2,1,0:T(8,128)}) custom-call(f32[16,8192]{1,0:T(8,128)} %refs_0_.2, s32[64,128]{1,0:T(8,128)} %bitcast.4, f32[16,64,512]{2,1,0:T(8,128)} %refs_16_.1, f32[16,64,64]{2,1,0:T(8,128)} %refs_14_.1, f32[1,64,64]{2,1,0:T(8,128)} %refs_15_.1, f32[16,2,64]{2,1,0:T(2,128)} %refs_10_.1, ...), custom_call_target="tpu_custom_call" | custom-call | tf_op jit(solution)/shard_map/up/pallas_call | solution.py:516
  9.9 7.3 %all-to-all-start = ((f32[32,24,128]{2,1,0:T(8,128)}), f32[32,24,128]{2,1,0:T(8,128)S(1)}, u32[]{:S(2)}, u32[]{:S(2)}) async-start(f32[32,24,128]{2,1,0:T(8,128)} %get-tuple-element.11), calls=%async_computation | async-start | bytes 786432 | tf_op jit(solution)/shard_map/all_to_all | solution.py:535
  17.2 0.3 collective-permute-start
  17.5 1.7 %collective-permute-start.1 = (f32[8,24,128]{2,1,0:T(8,128)}, f32[8,24,128]{2,1,0:T(8,128)S(1)}, u32[]{:S(2)}, u32[]{:S(2)}) collective-permute-start(f32[8,24,128]{2,1,0:T(8,128)} %get-tuple-element.10.refs_5_), channel_id=1, source_target_pairs={{0,2},{1,3},{2,0},{3,1},{4,6},{5,7},{6,4},{7,5},{8,10},{9,11},{10,... | collective-permute-start | bytes 294920 | tf_op jit(solution)/shard_map/ppermute | solution.py:537
  19.1 1.3 %collective-permute-start.2 = (f32[8,24,128]{2,1,0:T(8,128)}, f32[8,24,128]{2,1,0:T(8,128)S(1)}, u32[]{:S(2)}, u32[]{:S(2)}) collective-permute-start(f32[8,24,128]{2,1,0:T(8,128)} %get-tuple-element.10.refs_5_), channel_id=1, source_target_pairs={{0,3},{1,0},{2,1},{3,2},{4,7},{5,4},{6,5},{7,6},{8,11},{9,8},{10,9... | collective-permute-start | bytes 294920 | tf_op jit(solution)/shard_map/ppermute | solution.py:537
  21.1 23.4 %near.1 = (f32[16,16,512]{2,1,0:T(8,128)}, s32[64,128]{1,0:T(8,128)}) custom-call(s32[1]{0:T(128)} %bitcast.3.shift, f32[2,8192]{1,0:T(2,128)} %refs_0_.3, s32[64,128]{1,0:T(8,128)} %bitcast.5, f32[16,16,512]{2,1,0:T(8,128)} %get-tuple-element.12.refs_2_), custom_call_target="tpu_custom_call" | custom-call | flops 536870912 | bytes 1048576 | tf_op jit(solution)/shard_map/near/pallas_call | solution.py:541
  44.6 0.6 pad_add_fusion.refs_0_
  45.2 0.0 collective-permute-done.refs_6_
  45.2 0.0 copy-start.1
  45.2 0.0 collective-permute-done.1.refs_7_
  45.2 0.0 copy-start.2
  45.2 0.0 collective-permute-done.2.refs_8_
  45.2 0.0 copy-start.3
  45.2 0.0 all-to-all-done.refs_9_
  45.2 0.0 copy-start
  45.2 0.6 copy-done.1
  45.8 0.0 copy-done.2
  45.9 0.0 copy-done.3
  45.9 0.2 copy-done
  46.1 17.5 %far.1 = f32[16,8192]{1,0:T(8,128)} custom-call(s32[2]{0:T(128)} %pad_add_fusion.refs_0_, s32[16,16]{1,0:T(8,128)} %refs_1_.1, s32[16]{0:T(128)} %refs_2_.3, s32[1,8]{1,0:T(1,128)} %refs_3_.3, s32[1]{0:T(128)S(6)} %copy.15.refs_4_, f32[8,24,128]{2,1,0:T(8,128)} %get-tuple-element.10.refs_5_, f32[8,24,128]{2,1,0:T(8,128)} %copy-done.1, ...), custom_call_target="tpu_custom_call" | custom-call | tf_op jit(solution)/shard_map/far/pallas_call | solution.py:575
Async XLA Ops:
  9.9 35.3 %all-to-all-start = ((f32[32,24,128]{2,1,0:T(8,128)}), f32[32,24,128]{2,1,0:T(8,128)S(1)}, u32[]{:S(2)}, u32[]{:S(2)}) async-start(f32[32,24,128]{2,1,0:T(8,128)} %get-tuple-element.11), calls=%async_computation | async-start | bytes 786432 | tf_op jit(solution)/shard_map/all_to_all | solution.py:535
  17.2 28.0 %collective-permute-start = (f32[8,24,128]{2,1,0:T(8,128)}, f32[8,24,128]{2,1,0:T(8,128)S(1)}, u32[]{:S(2)}, u32[]{:S(2)}) collective-permute-start(f32[8,24,128]{2,1,0:T(8,128)} %get-tuple-element.10.refs_5_), channel_id=1, source_target_pairs={{0,1},{1,2},{2,3},{3,0},{4,5},{5,6},{6,7},{7,4},{8,9},{9,10},{10,1... | collective-permute-start | bytes 294920 | tf_op jit(solution)/shard_map/ppermute | solution.py:537
  17.5 27.7 %collective-permute-start.1 = (f32[8,24,128]{2,1,0:T(8,128)}, f32[8,24,128]{2,1,0:T(8,128)S(1)}, u32[]{:S(2)}, u32[]{:S(2)}) collective-permute-start(f32[8,24,128]{2,1,0:T(8,128)} %get-tuple-element.10.refs_5_), channel_id=1, source_target_pairs={{0,2},{1,3},{2,0},{3,1},{4,6},{5,7},{6,4},{7,5},{8,10},{9,11},{10,... | collective-permute-start | bytes 294920 | tf_op jit(solution)/shard_map/ppermute | solution.py:537
  19.1 26.0 %collective-permute-start.2 = (f32[8,24,128]{2,1,0:T(8,128)}, f32[8,24,128]{2,1,0:T(8,128)S(1)}, u32[]{:S(2)}, u32[]{:S(2)}) collective-permute-start(f32[8,24,128]{2,1,0:T(8,128)} %get-tuple-element.10.refs_5_), channel_id=1, source_target_pairs={{0,3},{1,0},{2,1},{3,2},{4,7},{5,4},{6,5},{7,6},{8,11},{9,8},{10,9... | collective-permute-start | bytes 294920 | tf_op jit(solution)/shard_map/ppermute | solution.py:537
  45.2 0.6 %copy-start.1 = (f32[8,24,128]{2,1,0:T(8,128)}, f32[8,24,128]{2,1,0:T(8,128)S(1)}, u32[]{:S(2)}) copy-start(f32[8,24,128]{2,1,0:T(8,128)S(1)} %collective-permute-done.refs_6_) | copy-start | bytes 294916
  45.2 0.7 %copy-start.2 = (f32[8,24,128]{2,1,0:T(8,128)}, f32[8,24,128]{2,1,0:T(8,128)S(1)}, u32[]{:S(2)}) copy-start(f32[8,24,128]{2,1,0:T(8,128)S(1)} %collective-permute-done.1.refs_7_) | copy-start | bytes 294916
  45.2 0.7 %copy-start.3 = (f32[8,24,128]{2,1,0:T(8,128)}, f32[8,24,128]{2,1,0:T(8,128)S(1)}, u32[]{:S(2)}) copy-start(f32[8,24,128]{2,1,0:T(8,128)S(1)} %collective-permute-done.2.refs_8_) | copy-start | bytes 294916
  45.2 0.8 %copy-start = (f32[32,24,128]{2,1,0:T(8,128)}, f32[32,24,128]{2,1,0:T(8,128)S(1)}, u32[]{:S(2)}) copy-start(f32[32,24,128]{2,1,0:T(8,128)S(1)} %all-to-all-done.refs_9_) | copy-start | bytes 1179652

commit v4 on v3

--- a/solution.py
+++ b/solution.py
@@ -3,7 +3,6 @@
 
 import jax
 import jax.numpy as jnp
-import ml_dtypes
 import numpy as np
 from jax import lax
 from jax.experimental import pallas as pl
@@ -18,7 +17,7 @@
 TINY = 1e-37
 PACK_ROWS = 24
 PART = 32
-AT_ONCE = 4
+AT_ONCE = 8
 
 
 def make_tables(norm):
@@ -186,23 +185,6 @@
     side = 128
     tiles = block // side
 
-    def three(row):
-        pieces = []
-        for _ in range(3):
-            pieces.append(row.astype(BF16).astype(F32))
-            row = row - pieces[-1]
-        return pieces
-
-    part = lax.broadcasted_iota(jnp.int32, (16, 3 * side), 0)
-    third = lax.broadcasted_iota(jnp.int32, (16, 3 * side), 1) // side
-    widen = jnp.where((part < 6) & (part // 3 == third), 1.0, 0.0)
-    left = np.float32(slope)
-    for each in range(3):
-        piece = np.float32(left.astype(ml_dtypes.bfloat16))
-        widen = jnp.where((part == 6 + each) & (third == 2), float(piece), widen)
-        left = left - piece
-    widen = widen.astype(BF16)
-
     def place_leaf(leaf, carry):
         index = leaf_index(perm, leaf, block)
         hot = one_hot(rows, index & (WIDE - 1))
@@ -225,15 +207,11 @@
         row_w = kind.astype(F32) * slope
         for place, row in enumerate((row_x, row_y, row_w)):
             across[leaf, place] = jnp.broadcast_to(row, (8, block))
-        stack = three(row_x) + three(row_y) + [kind.astype(F32)] * 3
-        stack = jnp.concatenate(stack + [jnp.zeros((7, block), F32)], axis=0).astype(BF16)
-        columns = dot(jnp.transpose(stack), widen)
-        for place in range(3):
-            column = columns[:, place * side : (place + 1) * side]
-            down[leaf, place] = column.reshape(block // 8, 8, side)
-        return carry
-
-    lax.fori_loop(0, leaves, place_leaf, 0, unroll=4)
+            turned = jnp.transpose(jnp.broadcast_to(row, (side, block)))
+            down[leaf, place] = turned.reshape(block // 8, 8, side)
+        return carry
+
+    lax.fori_loop(0, leaves, place_leaf, 0, unroll=2)
     inverse[...] = (slots[:chunks] + slots[chunks:] * WIDE).astype(jnp.int32)
     leave = pltpu.make_async_copy(inverse, inverse_out, sems.at[3])
     leave.start()
@@ -312,7 +290,8 @@
     given, out_at, held = refs[:10], refs[10], refs[11:21]
     leaf_all, source, coef, twice, cols, out, rows, srcs, dsts, sems = refs[21:]
     own = leaf_packs[0].shape[0]
-    owner = [lax.rem(place[1] - shift + groups, groups) for shift in range(groups)]
+    grp_pos = lax.rem(place[0], groups)
+    owner = [lax.rem(grp_pos - shift + groups, groups) for shift in range(groups)]
     arrive = [leaf_all.at[pl.ds(each * own, own)] for each in owner]
     copies = fetch(list(zip(leaf_packs + given, arrive + list(held))), sems)
     leaf_copies, copies = copies[:groups], [None] + copies[groups:]
@@ -327,7 +306,7 @@
     beside = 3 * groups
     sub_at = node_at + beside
     blank = sub_at + subtrees
-    sub_pos = place[0]
+    sub_pos = lax.div(place[0], groups)
     left = lax.broadcasted_iota(jnp.int32, (PACK_ROWS, 2 * rank), 1) < rank
 
     def list_leaf(leaf, at):
@@ -593,7 +572,7 @@
         compiler_params=params,
         name="far",
     )(
-        jnp.stack([sub_pos, lax.axis_index("grp")]).astype(jnp.int32),
+        device_pos.astype(jnp.int32).reshape(1),
         leaf_src,
         leaf_count,
         node_src,

time: 63.9 us -> 59.4 us (0.930)
  the two profiles are of different devices: /device:TPU:0 before, /device:TPU:1 now
where the time goes in v4:
time: 59.4 us; the launch traced here: 59.3 us
  Pallas kernels  48.4 us (81%)
  starting transfers between devices  9.33 us (16%)
  local copies, waits for them, and re-layouts  0.82 us (1%)
  between operations  0.75 us (1%)
    pallas_call x1, Pallas kernels, shards(): pl.pallas_call(near_kernel, out_shape=(jax.ShapeDtypeStruct((leaves, nvec...  21.4 us
    pallas_call x1, Pallas kernels, shards(): pl.pallas_call(functools.partial(far_kernel, groups, subtrees), out_shape...  17.1 us
    pallas_call x1, Pallas kernels, shards(): pl.pallas_call(up_kernel, out_shape=(jax.ShapeDtypeStruct((leaves, nvec,...  9.85 us
    all_to_all x1, starting transfers between devices, shards(): tree_all = lax.all_to_all(tree_pack, ('leaf', 'grp'), 0, 0, tiled=True)  7.1 us
    ppermute x3, starting transfers between devices, shards(): lax.ppermute(leaf_pack, 'grp', [(each, (each + shift) % groups) for each...  2.23 us
  transfers between devices with their start and end apart: 4, of which 0 were waited for; matrix products, arithmetic and copies ran while one was open for 0% of the time, Pallas kernels for 36%

profile of v4, /device:TPU:1, one launch (start us, length us, event | category | flops | bytes accessed | tf_op | source)
XLA Modules:
  0.0 59.3 jit_solution(10949836621090090206)
XLA Ops:
  0.0 9.9 %up.1 = (f32[16,16,512]{2,1,0:T(8,128)}, f32[8,24,128]{2,1,0:T(8,128)}, f32[32,24,128]{2,1,0:T(8,128)}) custom-call(f32[16,8192]{1,0:T(8,128)} %refs_0_.2, s32[64,128]{1,0:T(8,128)} %bitcast.3, f32[16,64,512]{2,1,0:T(8,128)} %refs_16_.1, f32[16,64,64]{2,1,0:T(8,128)} %refs_14_.1, f32[1,64,64]{2,1,0:T(8,128)} %refs_15_.1, f32[16,2,64]{2,1,0:T(2,128)} %refs_10_.1, ...), custom_call_target="tpu_custom_call" | custom-call | tf_op jit(solution)/shard_map/up/pallas_call | solution.py:495
  9.9 7.1 %all-to-all-start = ((f32[32,24,128]{2,1,0:T(8,128)}), f32[32,24,128]{2,1,0:T(8,128)S(1)}, u32[]{:S(2)}, u32[]{:S(2)}) async-start(f32[32,24,128]{2,1,0:T(8,128)} %get-tuple-element.11), calls=%async_computation | async-start | bytes 786432 | tf_op jit(solution)/shard_map/all_to_all | solution.py:514
  17.0 1.7 %collective-permute-start = (f32[8,24,128]{2,1,0:T(8,128)}, f32[8,24,128]{2,1,0:T(8,128)S(1)}, u32[]{:S(2)}, u32[]{:S(2)}) collective-permute-start(f32[8,24,128]{2,1,0:T(8,128)} %get-tuple-element.10.refs_5_), channel_id=1, source_target_pairs={{0,1},{1,2},{2,3},{3,0},{4,5},{5,6},{6,7},{7,4},{8,9},{9,10},{10,1... | collective-permute-start | bytes 294920 | tf_op jit(solution)/shard_map/ppermute | solution.py:516
  18.7 0.0 collective-permute-start.1
  18.7 0.5 collective-permute-start.2
  19.9 21.4 %near.1 = (f32[16,16,512]{2,1,0:T(8,128)}, s32[64,128]{1,0:T(8,128)}) custom-call(s32[1]{0:T(128)} %bitcast.2.shift, f32[2,8192]{1,0:T(2,128)} %refs_0_.3, s32[64,128]{1,0:T(8,128)} %bitcast.4, f32[16,16,512]{2,1,0:T(8,128)} %get-tuple-element.12.refs_2_), custom_call_target="tpu_custom_call" | custom-call | flops 536870912 | bytes 1048576 | tf_op jit(solution)/shard_map/near/pallas_call | solution.py:520
  41.3 0.0 collective-permute-done.refs_6_
  41.3 0.0 copy-start.1
  41.3 0.0 collective-permute-done.1.refs_7_
  41.3 0.0 copy-start.2
  41.3 0.0 collective-permute-done.2.refs_8_
  41.3 0.0 copy-start.3
  41.3 0.0 all-to-all-done.refs_9_
  41.4 0.0 copy-start
  41.4 0.6 copy-done.1
  41.9 0.0 copy-done.2
  42.0 0.0 copy-done.3
  42.0 0.2 copy-done
  42.2 17.1 %far.1 = f32[16,8192]{1,0:T(8,128)} custom-call(s32[1]{0:T(128)} %bitcast.refs_0_, s32[16,16]{1,0:T(8,128)} %refs_1_.1, s32[16]{0:T(128)} %refs_2_.3, s32[1,8]{1,0:T(1,128)} %refs_3_.3, s32[1]{0:T(128)S(6)} %copy.15.refs_4_, f32[8,24,128]{2,1,0:T(8,128)} %get-tuple-element.10.refs_5_, f32[8,24,128]{2,1,0:T(8,128)} %copy-done.1, f32[8,24,128]{2,1,0:T(8,128)} %copy-done.2, ...), custom_call_target="tpu_custom_call" | custom-call | tf_op jit(solution)/shard_map/far/pallas_call | solution.py:554
Async XLA Ops:
  9.9 31.5 %all-to-all-start = ((f32[32,24,128]{2,1,0:T(8,128)}), f32[32,24,128]{2,1,0:T(8,128)S(1)}, u32[]{:S(2)}, u32[]{:S(2)}) async-start(f32[32,24,128]{2,1,0:T(8,128)} %get-tuple-element.11), calls=%async_computation | async-start | bytes 786432 | tf_op jit(solution)/shard_map/all_to_all | solution.py:514
  17.0 24.3 %collective-permute-start = (f32[8,24,128]{2,1,0:T(8,128)}, f32[8,24,128]{2,1,0:T(8,128)S(1)}, u32[]{:S(2)}, u32[]{:S(2)}) collective-permute-start(f32[8,24,128]{2,1,0:T(8,128)} %get-tuple-element.10.refs_5_), channel_id=1, source_target_pairs={{0,1},{1,2},{2,3},{3,0},{4,5},{5,6},{6,7},{7,4},{8,9},{9,10},{10,1... | collective-permute-start | bytes 294920 | tf_op jit(solution)/shard_map/ppermute | solution.py:516
  18.7 22.6 %collective-permute-start.1 = (f32[8,24,128]{2,1,0:T(8,128)}, f32[8,24,128]{2,1,0:T(8,128)S(1)}, u32[]{:S(2)}, u32[]{:S(2)}) collective-permute-start(f32[8,24,128]{2,1,0:T(8,128)} %get-tuple-element.10.refs_5_), channel_id=1, source_target_pairs={{0,2},{1,3},{2,0},{3,1},{4,6},{5,7},{6,4},{7,5},{8,10},{9,11},{10,... | collective-permute-start | bytes 294920 | tf_op jit(solution)/shard_map/ppermute | solution.py:516
  18.7 22.6 %collective-permute-start.2 = (f32[8,24,128]{2,1,0:T(8,128)}, f32[8,24,128]{2,1,0:T(8,128)S(1)}, u32[]{:S(2)}, u32[]{:S(2)}) collective-permute-start(f32[8,24,128]{2,1,0:T(8,128)} %get-tuple-element.10.refs_5_), channel_id=1, source_target_pairs={{0,3},{1,0},{2,1},{3,2},{4,7},{5,4},{6,5},{7,6},{8,11},{9,8},{10,9... | collective-permute-start | bytes 294920 | tf_op jit(solution)/shard_map/ppermute | solution.py:516
  41.3 0.6 %copy-start.1 = (f32[8,24,128]{2,1,0:T(8,128)}, f32[8,24,128]{2,1,0:T(8,128)S(1)}, u32[]{:S(2)}) copy-start(f32[8,24,128]{2,1,0:T(8,128)S(1)} %collective-permute-done.refs_6_) | copy-start | bytes 294916
  41.3 0.7 %copy-start.2 = (f32[8,24,128]{2,1,0:T(8,128)}, f32[8,24,128]{2,1,0:T(8,128)S(1)}, u32[]{:S(2)}) copy-start(f32[8,24,128]{2,1,0:T(8,128)S(1)} %collective-permute-done.1.refs_7_) | copy-start | bytes 294916
  41.3 0.7 %copy-start.3 = (f32[8,24,128]{2,1,0:T(8,128)}, f32[8,24,128]{2,1,0:T(8,128)S(1)}, u32[]{:S(2)}) copy-start(f32[8,24,128]{2,1,0:T(8,128)S(1)} %collective-permute-done.2.refs_8_) | copy-start | bytes 294916
  41.4 0.8 %copy-start = (f32[32,24,128]{2,1,0:T(8,128)}, f32[32,24,128]{2,1,0:T(8,128)S(1)}, u32[]{:S(2)}) copy-start(f32[32,24,128]{2,1,0:T(8,128)S(1)} %all-to-all-done.refs_9_) | copy-start | bytes 1179652

commit v5 on v4

--- a/solution.py
+++ b/solution.py
@@ -161,8 +161,8 @@
 def near_kernel(shift, *refs):
     given, (near_out, inverse_out) = refs[:3], refs[3:5]
     held = refs[5:8]
-    near, inverse, flat, source, rows, across, down, slots = refs[8:16]
-    sooner, later, sems = refs[16:18], refs[18:20], refs[20]
+    near, inverse, flat, source, rows, slots = refs[8:14]
+    even, odd, sooner, later, sems = refs[14:16], refs[16:18], refs[18:20], refs[20:22], refs[22]
     copies = fetch(list(zip(given, held)), sems)
     crd, perm, tree_vec = held
     count_rows(rows)
@@ -185,7 +185,9 @@
     side = 128
     tiles = block // side
 
-    def place_leaf(leaf, carry):
+    def place_leaf(leaf, across, down):
+        live = jnp.where(leaf < leaves, 1.0, 0.0)
+        leaf = jnp.minimum(leaf, leaves - 1)
         index = leaf_index(perm, leaf, block)
         hot = one_hot(rows, index & (WIDE - 1))
         found = dot(source[...], hot)
@@ -194,8 +196,8 @@
         )
         mine = lax.broadcasted_iota(jnp.int32, (chunks, block), 0) == index >> SHIFT
         lane = lax.broadcasted_iota(jnp.int32, (chunks, block), 1) + leaf * block
-        lane_low = (lane & (WIDE - 1)).astype(F32)
-        lane_high = (lane >> SHIFT).astype(F32)
+        lane_low = (lane & (WIDE - 1)).astype(F32) * live
+        lane_high = (lane >> SHIFT).astype(F32) * live
         marks = jnp.concatenate(
             [jnp.where(mine, lane_low, 0.0), jnp.where(mine, lane_high, 0.0)], axis=0
         ).astype(BF16)
@@ -206,21 +208,16 @@
         kind = moved - 3 * ((moved * 43691) >> 17)
         row_w = kind.astype(F32) * slope
         for place, row in enumerate((row_x, row_y, row_w)):
-            across[leaf, place] = jnp.broadcast_to(row, (8, block))
+            across[place] = jnp.broadcast_to(row, (8, block))
             turned = jnp.transpose(jnp.broadcast_to(row, (side, block)))
-            down[leaf, place] = turned.reshape(block // 8, 8, side)
-        return carry
-
-    lax.fori_loop(0, leaves, place_leaf, 0, unroll=2)
-    inverse[...] = (slots[:chunks] + slots[chunks:] * WIDE).astype(jnp.int32)
-    leave = pltpu.make_async_copy(inverse, inverse_out, sems.at[3])
-    leave.start()
+            down[place] = turned.reshape(block // 8, 8, side)
+
     copies[2].wait()
 
-    def values(leaf, high, low):
+    def values(across, down, high, low):
         for col in range(tiles):
             cols = slice(col * side, (col + 1) * side)
-            over_x, over_y, over_w = [across[leaf, each, :, cols] for each in range(3)]
+            over_x, over_y, over_w = [across[each, :, cols] for each in range(3)]
             over_zero, over_one = over_w > 0.5 * slope, over_w > 1.5 * slope
 
             def across_table(power, first):
@@ -235,9 +232,9 @@
                 for part in range(side // PART):
                     first = row * side + part * PART
                     at = slice(first // 8, (first + PART) // 8)
-                    diff_x = down[leaf, 0, at] - over_x
-                    diff_y = down[leaf, 1, at] - over_y
-                    down_w = down[leaf, 2, at]
+                    diff_x = down[0, at] - over_x
+                    diff_y = down[1, at] - over_y
+                    down_w = down[2, at]
                     var_zero, var_one = down_w > 0.5 * slope, down_w > 1.5 * slope
                     square = (diff_x * diff_x + diff_y * diff_y) * (down_w + over_w)
                     arg = square * lax.rsqrt(TINY - square)
@@ -266,16 +263,23 @@
 
     def two_leaves(step, carry):
         apply(jnp.maximum(2 * step - 1, 0), *later)
-        values(2 * step, *sooner)
+        values(*even, *sooner)
+        place_leaf(2 * step + 1, *odd)
         apply(2 * step, *sooner)
-        values(2 * step + 1, *later)
-        return carry
+        values(*odd, *later)
+        place_leaf(2 * step + 2, *even)
+        return carry
+
+    place_leaf(0, *even)
 
     lax.fori_loop(0, leaves // 4, two_leaves, 0)
     half = slice(0, leaves // 2 - 1)
     first = pltpu.make_async_copy(near.at[half], near_out.at[half], sems.at[0])
     first.start()
     lax.fori_loop(leaves // 4, leaves // 2, two_leaves, 0)
+    inverse[...] = (slots[:chunks] + slots[chunks:] * WIDE).astype(jnp.int32)
+    leave = pltpu.make_async_copy(inverse, inverse_out, sems.at[3])
+    leave.start()
     apply(leaves - 1, *later)
     half = slice(leaves // 2 - 1, leaves)
     second = pltpu.make_async_copy(near.at[half], near_out.at[half], sems.at[1])
@@ -532,9 +536,12 @@
             pltpu.VMEM((2 * chunks, WIDE), F32),
             pltpu.VMEM((6 * chunks, WIDE), BF16),
             pltpu.VMEM((WIDE, block), jnp.int16),
-            pltpu.VMEM((leaves, 3, 8, block), F32),
-            pltpu.VMEM((leaves, 3, block // 8, 8, 128), F32),
             pltpu.VMEM((2 * chunks, WIDE), F32),
+            *[
+                pltpu.VMEM((3, 8, block), F32),
+                pltpu.VMEM((3, block // 8, 8, 128), F32),
+            ]
+            * 2,
             *[pltpu.VMEM((block, block), BF16)] * 4,
             pltpu.SemaphoreType.DMA((4,)),
         ],

time: 59.4 us -> 58.9 us (level)
  the two profiles are of different devices: /device:TPU:1 before, /device:TPU:0 now
where the time goes in v5:
time: 58.9 us; the launch traced here: 59.7 us
  Pallas kernels  47.5 us (81%)
  starting transfers between devices  10.6 us (18%)
  local copies, waits for them, and re-layouts  0.82 us (1%)
  between operations  0.75 us (1%)
    pallas_call x1, Pallas kernels, shards(): pl.pallas_call(near_kernel, out_shape=(jax.ShapeDtypeStruct((leaves, nvec...  20.5 us
    pallas_call x1, Pallas kernels, shards(): pl.pallas_call(functools.partial(far_kernel, groups, subtrees), out_shape...  17.1 us
    pallas_call x1, Pallas kernels, shards(): pl.pallas_call(up_kernel, out_shape=(jax.ShapeDtypeStruct((leaves, nvec,...  9.86 us
    all_to_all x1, starting transfers between devices, shards(): tree_all = lax.all_to_all(tree_pack, ('leaf', 'grp'), 0, 0, tiled=True)  7.3 us
    ppermute x3, starting transfers between devices, shards(): lax.ppermute(leaf_pack, 'grp', [(each, (each + shift) % groups) for each...  3.3 us
  transfers between devices with their start and end apart: 4, of which 0 were waited for; matrix products, arithmetic and copies ran while one was open for 0% of the time, Pallas kernels for 34%

profile of v5, /device:TPU:0, one launch (start us, length us, event | category | flops | bytes accessed | tf_op | source)
XLA Modules:
  0.0 59.7 jit_solution(10819621951501097499)
XLA Ops:
  0.0 9.9 %up.1 = (f32[16,16,512]{2,1,0:T(8,128)}, f32[8,24,128]{2,1,0:T(8,128)}, f32[32,24,128]{2,1,0:T(8,128)}) custom-call(f32[16,8192]{1,0:T(8,128)} %refs_0_.2, s32[64,128]{1,0:T(8,128)} %bitcast.3, f32[16,64,512]{2,1,0:T(8,128)} %refs_16_.1, f32[16,64,64]{2,1,0:T(8,128)} %refs_14_.1, f32[1,64,64]{2,1,0:T(8,128)} %refs_15_.1, f32[16,2,64]{2,1,0:T(2,128)} %refs_10_.1, ...), custom_call_target="tpu_custom_call" | custom-call | tf_op jit(solution)/shard_map/up/pallas_call | solution.py:499
  9.9 7.3 %all-to-all-start = ((f32[32,24,128]{2,1,0:T(8,128)}), f32[32,24,128]{2,1,0:T(8,128)S(1)}, u32[]{:S(2)}, u32[]{:S(2)}) async-start(f32[32,24,128]{2,1,0:T(8,128)} %get-tuple-element.11), calls=%async_computation | async-start | bytes 786432 | tf_op jit(solution)/shard_map/all_to_all | solution.py:518
  17.2 0.3 collective-permute-start
  17.5 1.7 %collective-permute-start.1 = (f32[8,24,128]{2,1,0:T(8,128)}, f32[8,24,128]{2,1,0:T(8,128)S(1)}, u32[]{:S(2)}, u32[]{:S(2)}) collective-permute-start(f32[8,24,128]{2,1,0:T(8,128)} %get-tuple-element.10.refs_5_), channel_id=1, source_target_pairs={{0,2},{1,3},{2,0},{3,1},{4,6},{5,7},{6,4},{7,5},{8,10},{9,11},{10,... | collective-permute-start | bytes 294920 | tf_op jit(solution)/shard_map/ppermute | solution.py:520
  19.1 1.3 %collective-permute-start.2 = (f32[8,24,128]{2,1,0:T(8,128)}, f32[8,24,128]{2,1,0:T(8,128)S(1)}, u32[]{:S(2)}, u32[]{:S(2)}) collective-permute-start(f32[8,24,128]{2,1,0:T(8,128)} %get-tuple-element.10.refs_5_), channel_id=1, source_target_pairs={{0,3},{1,0},{2,1},{3,2},{4,7},{5,4},{6,5},{7,6},{8,11},{9,8},{10,9... | collective-permute-start | bytes 294920 | tf_op jit(solution)/shard_map/ppermute | solution.py:520
  21.1 20.5 %near.1 = (f32[16,16,512]{2,1,0:T(8,128)}, s32[64,128]{1,0:T(8,128)}) custom-call(s32[1]{0:T(128)} %bitcast.2.shift, f32[2,8192]{1,0:T(2,128)} %refs_0_.3, s32[64,128]{1,0:T(8,128)} %bitcast.4, f32[16,16,512]{2,1,0:T(8,128)} %get-tuple-element.12.refs_2_), custom_call_target="tpu_custom_call" | custom-call | flops 536870912 | bytes 1048576 | tf_op jit(solution)/shard_map/near/pallas_call | solution.py:524
  41.7 0.0 collective-permute-done.refs_6_
  41.7 0.0 copy-start.1
  41.7 0.0 collective-permute-done.1.refs_7_
  41.7 0.0 copy-start.2
  41.7 0.0 collective-permute-done.2.refs_8_
  41.7 0.0 copy-start.3
  41.7 0.0 all-to-all-done.refs_9_
  41.7 0.0 copy-start
  41.8 0.6 copy-done.1
  42.3 0.0 copy-done.2
  42.4 0.0 copy-done.3
  42.4 0.2 copy-done
  42.6 17.1 %far.1 = f32[16,8192]{1,0:T(8,128)} custom-call(s32[1]{0:T(128)} %bitcast.refs_0_, s32[16,16]{1,0:T(8,128)} %refs_1_.1, s32[16]{0:T(128)} %refs_2_.3, s32[1,8]{1,0:T(1,128)} %refs_3_.3, s32[1]{0:T(128)S(6)} %copy.15.refs_4_, f32[8,24,128]{2,1,0:T(8,128)} %get-tuple-element.10.refs_5_, f32[8,24,128]{2,1,0:T(8,128)} %copy-done.1, f32[8,24,128]{2,1,0:T(8,128)} %copy-done.2, ...), custom_call_target="tpu_custom_call" | custom-call | tf_op jit(solution)/shard_map/far/pallas_call | solution.py:561
Async XLA Ops:
  9.9 31.9 %all-to-all-start = ((f32[32,24,128]{2,1,0:T(8,128)}), f32[32,24,128]{2,1,0:T(8,128)S(1)}, u32[]{:S(2)}, u32[]{:S(2)}) async-start(f32[32,24,128]{2,1,0:T(8,128)} %get-tuple-element.11), calls=%async_computation | async-start | bytes 786432 | tf_op jit(solution)/shard_map/all_to_all | solution.py:518
  17.2 24.5 %collective-permute-start = (f32[8,24,128]{2,1,0:T(8,128)}, f32[8,24,128]{2,1,0:T(8,128)S(1)}, u32[]{:S(2)}, u32[]{:S(2)}) collective-permute-start(f32[8,24,128]{2,1,0:T(8,128)} %get-tuple-element.10.refs_5_), channel_id=1, source_target_pairs={{0,1},{1,2},{2,3},{3,0},{4,5},{5,6},{6,7},{7,4},{8,9},{9,10},{10,1... | collective-permute-start | bytes 294920 | tf_op jit(solution)/shard_map/ppermute | solution.py:520
  17.5 24.2 %collective-permute-start.1 = (f32[8,24,128]{2,1,0:T(8,128)}, f32[8,24,128]{2,1,0:T(8,128)S(1)}, u32[]{:S(2)}, u32[]{:S(2)}) collective-permute-start(f32[8,24,128]{2,1,0:T(8,128)} %get-tuple-element.10.refs_5_), channel_id=1, source_target_pairs={{0,2},{1,3},{2,0},{3,1},{4,6},{5,7},{6,4},{7,5},{8,10},{9,11},{10,... | collective-permute-start | bytes 294920 | tf_op jit(solution)/shard_map/ppermute | solution.py:520
  19.1 22.6 %collective-permute-start.2 = (f32[8,24,128]{2,1,0:T(8,128)}, f32[8,24,128]{2,1,0:T(8,128)S(1)}, u32[]{:S(2)}, u32[]{:S(2)}) collective-permute-start(f32[8,24,128]{2,1,0:T(8,128)} %get-tuple-element.10.refs_5_), channel_id=1, source_target_pairs={{0,3},{1,0},{2,1},{3,2},{4,7},{5,4},{6,5},{7,6},{8,11},{9,8},{10,9... | collective-permute-start | bytes 294920 | tf_op jit(solution)/shard_map/ppermute | solution.py:520
  41.7 0.6 %copy-start.1 = (f32[8,24,128]{2,1,0:T(8,128)}, f32[8,24,128]{2,1,0:T(8,128)S(1)}, u32[]{:S(2)}) copy-start(f32[8,24,128]{2,1,0:T(8,128)S(1)} %collective-permute-done.refs_6_) | copy-start | bytes 294916
  41.7 0.7 %copy-start.2 = (f32[8,24,128]{2,1,0:T(8,128)}, f32[8,24,128]{2,1,0:T(8,128)S(1)}, u32[]{:S(2)}) copy-start(f32[8,24,128]{2,1,0:T(8,128)S(1)} %collective-permute-done.1.refs_7_) | copy-start | bytes 294916
  41.7 0.7 %copy-start.3 = (f32[8,24,128]{2,1,0:T(8,128)}, f32[8,24,128]{2,1,0:T(8,128)S(1)}, u32[]{:S(2)}) copy-start(f32[8,24,128]{2,1,0:T(8,128)S(1)} %collective-permute-done.2.refs_8_) | copy-start | bytes 294916
  41.7 0.8 %copy-start = (f32[32,24,128]{2,1,0:T(8,128)}, f32[32,24,128]{2,1,0:T(8,128)S(1)}, u32[]{:S(2)}) copy-start(f32[32,24,128]{2,1,0:T(8,128)S(1)} %all-to-all-done.refs_9_) | copy-start | bytes 1179652
